TPU v7x, 512 devices: a whole 4x8x8 slice. The times are simulated.
512 devices in a mesh: wide: 64 (over y, z), narrow: 8 (over x, core).
Axes of the slice: x: 4, y: 8, z: 8, core: 2. Of those that a mesh axis runs over, the one named last changes fastest.
Arguments:
- pressure: float32 [512, 512, 512], P('wide', 'narrow'), may hold values from -6 to 6
Outputs:
- detail_one: float32 [7, 256, 256, 256], P(None, 'wide', 'narrow')
- detail_two: float32 [7, 128, 128, 128], P(None, 'wide', 'narrow')
- detail_three: float32 [7, 64, 64, 64], P(None, 'wide', 'narrow')
- bands_four: float32 [8, 32, 32, 32], P(None, None, 'narrow')
All inputs are finite; a program needn't handle non-finite values.
Results may differ from a plain program's by a relative error of at most 0.00016.
Values sent between devices are 32-bit elements; how exact they have to be, the bound alone decides.
A program may use at most 64 MiB of HBM per device.

v0:
```python
import jax
import jax.numpy as jnp
from jax import lax
from jax.sharding import PartitionSpec as P

LEVELS = 4


LIFT_ALPHA = -1.586134342
LIFT_BETA = -0.05298011854
LIFT_GAMMA = 0.8829110762
LIFT_DELTA = 0.4435068522
LIFT_ZETA = 1.149604398
LIFT_INVERSE = 1.0 / 1.149604398


def extended(cells, sides, width):
    for axis, dim in sides:
        count = lax.axis_size(axis)
        ends = count - 1
        head = lax.slice_in_dim(cells, 0, width, axis=dim)
        tail = lax.slice_in_dim(cells, cells.shape[dim] - width, cells.shape[dim], axis=dim)
        cells = jnp.concatenate(
            [
                lax.ppermute(tail, axis, [(i, (i + 1) % count) for i in range(ends)]),
                cells,
                lax.ppermute(head, axis, [((i + 1) % count, i) for i in range(ends)]),
            ],
            axis=dim,
        )
    return cells


def shifted(value, axis, steps):
    count = lax.axis_size(axis)
    first, last = (max(0, -steps), min(count, count - steps))
    return lax.ppermute(value, axis, [(source, source + steps) for source in range(first, last)])


def in_order(blocks, dim):
    blocks = jnp.moveaxis(blocks, 0, dim)
    shape = blocks.shape
    return blocks.reshape(*shape[:dim], shape[dim] * shape[dim + 1], *shape[dim + 2 :])


def from_everyone(shard, axis):
    devices = lax.axis_size(axis)
    return lax.all_to_all(
        jnp.broadcast_to(shard[None], (devices, *shard.shape)), axis, 0, 0, tiled=True
    )


def collect(shard, axis, dim):
    return in_order(from_everyone(shard, axis), dim)


def keep_same(piece):
    return piece


def lift_general(volume, along, pull_next, pull_prev, at_first, at_last):
    length = volume.shape[along]
    half = length // 2
    even_part = lax.slice_in_dim(volume, 0, length, 2, along)
    odd_part = lax.slice_in_dim(volume, 1, length, 2, along)

    def next_even(source):
        edge = lax.slice_in_dim(source, half - 1, half, 1, along)
        outer = jnp.where(at_last, edge, pull_next(lax.slice_in_dim(source, 0, 1, 1, along)))
        return jnp.concatenate([lax.slice_in_dim(source, 1, half, 1, along), outer], along)

    def prev_odd(source):
        edge = lax.slice_in_dim(source, 0, 1, 1, along)
        outer = jnp.where(
            at_first, edge, pull_prev(lax.slice_in_dim(source, half - 1, half, 1, along))
        )
        return jnp.concatenate([outer, lax.slice_in_dim(source, 0, half - 1, 1, along)], along)

    odd_part = odd_part + LIFT_ALPHA * (even_part + next_even(even_part))
    even_part = even_part + LIFT_BETA * (prev_odd(odd_part) + odd_part)
    odd_part = odd_part + LIFT_GAMMA * (even_part + next_even(even_part))
    even_part = even_part + LIFT_DELTA * (prev_odd(odd_part) + odd_part)
    return jnp.stack([even_part * LIFT_ZETA, odd_part * LIFT_INVERSE], 0)


def lift_local(volume, along):
    return lift_general(volume, along, keep_same, keep_same, True, True)


def lift_columns(volume):
    width = volume.shape[2]
    unit_matrix = jnp.eye(width, dtype=jnp.float32)
    lift_table = lift_local(unit_matrix, 1)
    return jnp.einsum("zyi,bij->bzyj", volume, lift_table, precision=lax.Precision.HIGHEST)


def lift_widened(widened, along, at_first, at_last):
    total = widened.shape[along]
    left_mirror = jnp.flip(lax.slice_in_dim(widened, 5, 9, 1, along), along)
    right_mirror = jnp.flip(lax.slice_in_dim(widened, total - 9, total - 5, 1, along), along)
    left_part = jnp.where(at_first, left_mirror, lax.slice_in_dim(widened, 0, 4, 1, along))
    right_part = jnp.where(
        at_last, right_mirror, lax.slice_in_dim(widened, total - 4, total, 1, along)
    )
    middle = lax.slice_in_dim(widened, 4, total - 4, 1, along)
    filled = jnp.concatenate([left_part, middle, right_part], along)
    lifted = lift_local(filled, along)
    owned = (total - 8) // 2
    return lax.slice_in_dim(lifted, 2, 2 + owned, 1, along + 1)


def widen_rows(piece):
    return extended(piece, (("narrow", 2),), 4)


def widen_planes(piece):
    return extended(piece, (("wide", 2),), 4)


def pull_next_y(piece):
    return shifted(piece, "narrow", -1)


def pull_prev_y(piece):
    return shifted(piece, "narrow", 1)


def pull_next_z(piece):
    return shifted(piece, "wide", -1)


def pull_prev_z(piece):
    return shifted(piece, "wide", 1)


def per_device(pressure):
    wide_index = lax.axis_index("wide")
    narrow_index = lax.axis_index("narrow")
    wide_count = lax.axis_size("wide")
    wide_first = wide_index == 0
    wide_last = wide_index == wide_count - 1
    narrow_first = narrow_index == 0
    narrow_last = narrow_index == lax.axis_size("narrow") - 1
    volume = pressure
    details = []
    for _ in range(LEVELS - 1):
        planes_here = volume.shape[0]
        x_pair = lift_columns(volume)
        y_pair = lift_widened(widen_rows(x_pair), 2, narrow_first, narrow_last)
        if planes_here >= 4:
            z_pair = lift_widened(widen_planes(y_pair), 2, wide_first, wide_last)
        else:
            z_pair = lift_general(y_pair, 2, pull_next_z, pull_prev_z, wide_first, wide_last)
        band_set = z_pair.reshape((8,) + z_pair.shape[3:])
        details.append(band_set[1:])
        volume = band_set[0]
    whole = collect(volume, "wide", 0)
    x_pair = lift_columns(whole)
    y_pair = lift_general(x_pair, 2, pull_next_y, pull_prev_y, narrow_first, narrow_last)
    z_pair = lift_local(y_pair, 2)
    last_bands = z_pair.reshape((8,) + z_pair.shape[3:])
    return (details[0], details[1], details[2], last_bands)


def solution(mesh):
    in_specs = (P("wide", "narrow", None),)
    out_specs = (
        P(None, "wide", "narrow", None),
        P(None, "wide", "narrow", None),
        P(None, "wide", "narrow", None),
        P(None, None, "narrow", None),
    )
    return jax.shard_map(
        per_device, mesh=mesh, in_specs=in_specs, out_specs=out_specs, check_vma=False
    )
```

profile of v0, /device:TPU:1, one launch (start us, length us, event | category | flops | bytes accessed | tf_op | source)
XLA Modules:
  0.0 206.0 jit_solution(16792480175275900303)
XLA Ops:
  0.8 19.5 %slice.508 = f32[512,256]{1,0:T(8,128)S(1)} slice(f32[512,512]{1,0:T(8,128)S(1)} %fusion.14), slice={[0:512:1], [1:512:2]} | slice | bytes 1048576 | tf_op jit(solution)/shard_map/slice | solution.py:65
  20.2 19.5 %slice.507 = f32[512,256]{1,0:T(8,128)S(1)} slice(f32[512,512]{1,0:T(8,128)S(1)} %fusion.14), slice={[0:512:1], [0:512:2]} | slice | bytes 1048576 | tf_op jit(solution)/shard_map/slice | solution.py:64
  41.2 1.9 convolution_bitcast_fusion
  43.1 8.8 %collective-permute-start.1 = (f32[2,8,4,256]{3,2,1,0:T(4,128)S(1)}, f32[2,8,4,256]{3,2,1,0:T(4,128)S(1)}, u32[]{:S(2)}, u32[]{:S(2)}) collective-permute-start(f32[2,8,4,256]{3,2,1,0:T(4,128)S(1)} %get-tuple-element.41), channel_id=1, source_target_pairs={{1,0},{2,1},{3,2},{4,3},{5,4},{6,5},{7,6},{9,8},{10,9},{11,10},{12... | collective-permute-start | bytes 196616 | tf_op jit(solution)/shard_map/ppermute | solution.py:27
  51.9 2.1 %collective-permute-start = (f32[2,8,4,256]{3,2,1,0:T(4,128)S(1)}, f32[2,8,4,256]{3,2,1,0:T(4,128)S(1)}, u32[]{:S(2)}, u32[]{:S(2)}) collective-permute-start(f32[2,8,4,256]{3,2,1,0:T(4,128)S(1)} %get-tuple-element.40), channel_id=1, source_target_pairs={{0,1},{1,2},{2,3},{3,4},{4,5},{5,6},{6,7},{8,9},{9,10},{10,11},{11... | collective-permute-start | bytes 196616 | tf_op jit(solution)/shard_map/ppermute | solution.py:25
  54.1 4.5 %slice.549 = f32[256,128]{1,0:T(8,128)S(1)} slice(f32[256,256]{1,0:T(8,128)S(1)} %fusion.52), slice={[0:256:1], [1:256:2]} | slice | bytes 262144 | tf_op jit(solution)/shard_map/slice | solution.py:65
  58.6 4.5 %slice.548 = f32[256,128]{1,0:T(8,128)S(1)} slice(f32[256,256]{1,0:T(8,128)S(1)} %fusion.52), slice={[0:256:1], [0:256:2]} | slice | bytes 262144 | tf_op jit(solution)/shard_map/slice | solution.py:64
  63.6 0.8 slice.693
  67.0 2.2 %slice.522 = f32[2,8,36,256]{3,2,1,0:T(8,128)} slice(f32[2,8,72,256]{3,2,1,0:T(8,128)S(1)} %pad_maximum_fusion.1), slice={[0:2:1], [0:8:1], [1:72:2], [0:256:1]} | slice | bytes 1179648 | tf_op jit(solution)/shard_map/slice | solution.py:65
  69.2 1.0 copy-done.1
  71.2 1.3 collective-permute-start.3
  72.6 4.0 %collective-permute-start.2 = (f32[2,2,4,32,256]{4,3,2,1,0:T(8,128)S(1)}, f32[2,2,4,32,256]{4,3,2,1,0:T(8,128)S(1)}, u32[]{:S(2)}, u32[]{:S(2)}) collective-permute-start(f32[2,2,4,32,256]{4,3,2,1,0:T(8,128)S(1)} %get-tuple-element.37), channel_id=1, source_target_pairs={{0,8},{8,16},{16,24},{24,32},{32,40},{40,48},{48,56},{56,64},{64,7... | collective-permute-start | bytes 1572872 | tf_op jit(solution)/shard_map/ppermute | solution.py:25
  76.9 9.2 %collective-permute-done.3 = f32[2,2,4,32,256]{4,3,2,1,0:T(8,128)S(1)} collective-permute-done((f32[2,2,4,32,256]{4,3,2,1,0:T(8,128)S(1)}, f32[2,2,4,32,256]{4,3,2,1,0:T(8,128)S(1)}, u32[]{:S(2)}, u32[]{:S(2)}) %collective-permute-start.3) | collective-permute-done | bytes 524320 | tf_op jit(solution)/shard_map/ppermute | solution.py:27
  86.1 0.9 collective-permute-done.2
  89.6 3.6 %collective-permute-start.5 = (f32[2,4,4,128]{3,2,1,0:T(4,128)S(1)}, f32[2,4,4,128]{3,2,1,0:T(4,128)S(1)}, u32[]{:S(2)}, u32[]{:S(2)}) collective-permute-start(f32[2,4,4,128]{3,2,1,0:T(4,128)S(1)} %get-tuple-element.47), channel_id=1, source_target_pairs={{1,0},{2,1},{3,2},{4,3},{5,4},{6,5},{7,6},{9,8},{10,9},{11,10},{12... | collective-permute-start | bytes 49160 | tf_op jit(solution)/shard_map/ppermute | solution.py:27
  93.3 2.0 collective-permute-start.4
  95.3 1.1 collective-permute-done.4
  96.9 1.3 collective-permute-start.6
  98.2 4.7 %collective-permute-start.7 = (f32[2,2,4,16,128]{4,3,2,1,0:T(8,128)S(1)}, f32[2,2,4,16,128]{4,3,2,1,0:T(8,128)S(1)}, u32[]{:S(2)}, u32[]{:S(2)}) collective-permute-start(f32[2,2,4,16,128]{4,3,2,1,0:T(8,128)S(1)} %pad_maximum_fusion.11), channel_id=1, source_target_pairs={{0,8},{8,16},{16,24},{24,32},{32,40},{40,48},{48,56},{56,64},{64,7... | collective-permute-start | bytes 393224 | tf_op jit(solution)/shard_map/ppermute | solution.py:25
  102.9 1.7 collective-permute-done.6
  104.7 0.9 collective-permute-done.7
  106.4 2.9 %collective-permute-start.9 = (f32[2,2,4,64]{3,2,1,0:T(4,128)S(1)}, f32[2,2,4,64]{3,2,1,0:T(4,128)S(1)}, u32[]{:S(2)}, u32[]{:S(2)}) collective-permute-start(f32[2,2,4,64]{3,2,1,0:T(4,128)S(1)} %get-tuple-element.51), channel_id=1, source_target_pairs={{1,0},{2,1},{3,2},{4,3},{5,4},{6,5},{7,6},{9,8},{10,9},{11,10},{12... | collective-permute-start | bytes 12296 | tf_op jit(solution)/shard_map/ppermute | solution.py:27
  109.4 3.1 %collective-permute-start.8 = (f32[2,2,4,64]{3,2,1,0:T(4,128)S(1)}, f32[2,2,4,64]{3,2,1,0:T(4,128)S(1)}, u32[]{:S(2)}, u32[]{:S(2)}) collective-permute-start(f32[2,2,4,64]{3,2,1,0:T(4,128)S(1)} %get-tuple-element.50), channel_id=1, source_target_pairs={{0,1},{1,2},{2,3},{3,4},{4,5},{5,6},{6,7},{8,9},{9,10},{10,11},{11... | collective-permute-start | bytes 12296 | tf_op jit(solution)/shard_map/ppermute | solution.py:25
  112.5 0.7 collective-permute-done.8
  113.6 1.3 collective-permute-start.10
  114.9 3.9 %collective-permute-done.10 = f32[2,2,1,8,64]{4,3,1,0,2:T(8,128)S(1)} collective-permute-done((f32[2,2,1,8,64]{4,3,1,0,2:T(8,128)S(1)}, f32[2,2,1,8,64]{4,3,1,0,2:T(8,128)S(1)}, u32[]{:S(2)}, u32[]{:S(2)}) %collective-permute-start.10) | collective-permute-done | bytes 8224 | tf_op jit(solution)/shard_map/ppermute | solution.py:37
  118.8 3.6 %collective-permute-start.11 = (f32[2,2,1,8,64]{4,3,1,0,2:T(8,128)S(1)}, f32[2,2,1,8,64]{4,3,1,0,2:T(8,128)S(1)}, u32[]{:S(2)}, u32[]{:S(2)}) collective-permute-start(f32[2,2,1,8,64]{4,3,1,0,2:T(8,128)S(1)} %bitcast.184), channel_id=1, source_target_pairs={{0,8},{8,16},{16,24},{24,32},{32,40},{40,48},{48,56},{56,64},{64,7... | collective-permute-start | bytes 24584 | tf_op jit(solution)/shard_map/ppermute | solution.py:37
  122.5 0.8 collective-permute-done.11
  123.3 1.3 collective-permute-start.12
  124.6 3.8 %collective-permute-done.12 = f32[2,2,1,8,64]{4,3,1,0,2:T(8,128)S(1)} collective-permute-done((f32[2,2,1,8,64]{4,3,1,0,2:T(8,128)S(1)}, f32[2,2,1,8,64]{4,3,1,0,2:T(8,128)S(1)}, u32[]{:S(2)}, u32[]{:S(2)}) %collective-permute-start.12) | collective-permute-done | bytes 8224 | tf_op jit(solution)/shard_map/ppermute | solution.py:37
  128.5 5.3 %collective-permute-start.13 = (f32[2,2,1,8,64]{4,3,1,0,2:T(8,128)S(1)}, f32[2,2,1,8,64]{4,3,1,0,2:T(8,128)S(1)}, u32[]{:S(2)}, u32[]{:S(2)}) collective-permute-start(f32[2,2,1,8,64]{4,3,1,0,2:T(8,128)S(1)} %bitcast.194), channel_id=1, source_target_pairs={{0,8},{8,16},{16,24},{24,32},{32,40},{40,48},{48,56},{56,64},{64,7... | collective-permute-start | bytes 24584 | tf_op jit(solution)/shard_map/ppermute | solution.py:37
  133.8 0.8 collective-permute-done.13
  134.7 0.8 reshape.38
  135.5 24.5 %all-to-all-start = ((f32[64,1,512]{2,1,0:T(1,128)}), f32[64,1,512]{2,1,0:T(1,128)S(1)}, u32[]{:S(2)}, u32[]{:S(2)}) async-start(f32[64,1,512]{2,1,0:T(1,128)} %reshape.38), calls=%async_computation | async-start | bytes 262144 | tf_op jit(solution)/shard_map/all_to_all | solution.py:48
  160.1 11.2 %all-to-all-done = f32[64,1,512]{2,1,0:T(1,128)S(1)} async-done(((f32[64,1,512]{2,1,0:T(1,128)}), f32[64,1,512]{2,1,0:T(1,128)S(1)}, u32[]{:S(2)}, u32[]{:S(2)}) %all-to-all-start) | async-done | bytes 131104 | tf_op jit(solution)/shard_map/all_to_all | solution.py:48
  171.8 0.9 reduce
  172.9 0.9 convolution_bitcast_fusion.1
  173.8 6.6 %collective-permute-start.14 = (f32[2,64,1,32]{1,3,2,0:T(8,128)S(1)}, f32[2,64,1,32]{1,3,2,0:T(8,128)S(1)}, u32[]{:S(2)}, u32[]{:S(2)}) collective-permute-start(f32[2,64,1,32]{1,3,2,0:T(8,128)S(1)} %slice.751), channel_id=1, source_target_pairs={{1,0},{2,1},{3,2},{4,3},{5,4},{6,5},{7,6},{9,8},{10,9},{11,10},{12... | collective-permute-start | bytes 49160 | tf_op jit(solution)/shard_map/ppermute | solution.py:37
  180.4 5.2 %collective-permute-done.14 = f32[2,64,1,32]{1,3,2,0:T(8,128)S(1)} collective-permute-done((f32[2,64,1,32]{1,3,2,0:T(8,128)S(1)}, f32[2,64,1,32]{1,3,2,0:T(8,128)S(1)}, u32[]{:S(2)}, u32[]{:S(2)}) %collective-permute-start.14) | collective-permute-done | bytes 16416 | tf_op jit(solution)/shard_map/ppermute | solution.py:37
  185.6 1.9 collective-permute-start.15
  187.6 1.2 collective-permute-done.15
  188.8 2.1 %collective-permute-start.16 = (f32[2,64,1,32]{1,3,2,0:T(8,128)S(1)}, f32[2,64,1,32]{1,3,2,0:T(8,128)S(1)}, u32[]{:S(2)}, u32[]{:S(2)}) collective-permute-start(f32[2,64,1,32]{1,3,2,0:T(8,128)S(1)} %slice.757), channel_id=1, source_target_pairs={{1,0},{2,1},{3,2},{4,3},{5,4},{6,5},{7,6},{9,8},{10,9},{11,10},{12... | collective-permute-start | bytes 49160 | tf_op jit(solution)/shard_map/ppermute | solution.py:37
  190.9 3.5 %collective-permute-done.16 = f32[2,64,1,32]{1,3,2,0:T(8,128)S(1)} collective-permute-done((f32[2,64,1,32]{1,3,2,0:T(8,128)S(1)}, f32[2,64,1,32]{1,3,2,0:T(8,128)S(1)}, u32[]{:S(2)}, u32[]{:S(2)}) %collective-permute-start.16) | collective-permute-done | bytes 16416 | tf_op jit(solution)/shard_map/ppermute | solution.py:37
  194.5 1.9 collective-permute-start.17
  196.4 1.0 slice.687
  198.8 2.5 %slice.642 = f32[2,2,32,4,32]{2,4,3,1,0:T(8,128)S(1)} slice(f32[2,2,64,4,32]{2,4,3,1,0:T(8,128)S(1)} %pad_maximum_fusion.6), slice={[0:2:1], [0:2:1], [1:64:2], [0:4:1], [0:32:1]} | slice | bytes 131072 | tf_op jit(solution)/shard_map/slice | solution.py:65
  201.3 2.5 %slice.641 = f32[2,2,32,4,32]{2,4,3,1,0:T(8,128)S(1)} slice(f32[2,2,64,4,32]{2,4,3,1,0:T(8,128)S(1)} %pad_maximum_fusion.6), slice={[0:2:1], [0:2:1], [0:64:2], [0:4:1], [0:32:1]} | slice | bytes 131072 | tf_op jit(solution)/shard_map/slice | solution.py:64
  205.0 1.0 copy.27
  (199 shorter events, 13.3 us)
Async XLA Ops:
  0.6 40.6 %copy-start = (f32[8,64,512]{2,1,0:T(8,128)S(1)}, f32[8,64,512]{2,1,0:T(8,128)}, u32[]{:S(2)}) copy-start(f32[8,64,512]{2,1,0:T(8,128)} %param.1) | copy-start | bytes 3145732
  43.1 22.9 %collective-permute-start.1 = (f32[2,8,4,256]{3,2,1,0:T(4,128)S(1)}, f32[2,8,4,256]{3,2,1,0:T(4,128)S(1)}, u32[]{:S(2)}, u32[]{:S(2)}) collective-permute-start(f32[2,8,4,256]{3,2,1,0:T(4,128)S(1)} %get-tuple-element.41), channel_id=1, source_target_pairs={{1,0},{2,1},{3,2},{4,3},{5,4},{6,5},{7,6},{9,8},{10,9},{11,10},{12... | collective-permute-start | bytes 196616 | tf_op jit(solution)/shard_map/ppermute | solution.py:27
  51.9 14.2 %collective-permute-start = (f32[2,8,4,256]{3,2,1,0:T(4,128)S(1)}, f32[2,8,4,256]{3,2,1,0:T(4,128)S(1)}, u32[]{:S(2)}, u32[]{:S(2)}) collective-permute-start(f32[2,8,4,256]{3,2,1,0:T(4,128)S(1)} %get-tuple-element.40), channel_id=1, source_target_pairs={{0,1},{1,2},{2,3},{3,4},{4,5},{5,6},{6,7},{8,9},{9,10},{10,11},{11... | collective-permute-start | bytes 196616 | tf_op jit(solution)/shard_map/ppermute | solution.py:25
  63.4 2.8 %copy-start.6 = (f32[128,64]{0,1:T(8,128)}, f32[128,64]{0,1:T(8,128)S(1)}, u32[]{:S(2)}) copy-start(f32[128,64]{0,1:T(8,128)S(1)} %fusion.97) | copy-start | bytes 98308
  63.6 2.5 %copy-start.2 = (f32[128,64]{0,1:T(8,128)}, f32[128,64]{0,1:T(8,128)S(1)}, u32[]{:S(2)}) copy-start(f32[128,64]{0,1:T(8,128)S(1)} %fusion.99) | copy-start | bytes 98308
  69.1 1.1 copy-start.1
  71.0 1.5 copy-start.4
  71.0 1.5 copy-start.5
  71.2 14.9 %collective-permute-start.3 = (f32[2,2,4,32,256]{4,3,2,1,0:T(8,128)S(1)}, f32[2,2,4,32,256]{4,3,2,1,0:T(8,128)S(1)}, u32[]{:S(2)}, u32[]{:S(2)}) collective-permute-start(f32[2,2,4,32,256]{4,3,2,1,0:T(8,128)S(1)} %get-tuple-element.38), channel_id=1, source_target_pairs={{8,0},{16,8},{24,16},{32,24},{40,32},{48,40},{56,48},{64,56},{72,6... | collective-permute-start | bytes 1572872 | tf_op jit(solution)/shard_map/ppermute | solution.py:27
  72.6 14.4 %collective-permute-start.2 = (f32[2,2,4,32,256]{4,3,2,1,0:T(8,128)S(1)}, f32[2,2,4,32,256]{4,3,2,1,0:T(8,128)S(1)}, u32[]{:S(2)}, u32[]{:S(2)}) collective-permute-start(f32[2,2,4,32,256]{4,3,2,1,0:T(8,128)S(1)} %get-tuple-element.37), channel_id=1, source_target_pairs={{0,8},{8,16},{16,24},{24,32},{32,40},{40,48},{48,56},{56,64},{64,7... | collective-permute-start | bytes 1572872 | tf_op jit(solution)/shard_map/ppermute | solution.py:25
  89.1 4.0 %copy-start.3 = (f32[128,64]{0,1:T(8,128)S(1)}, f32[128,64]{0,1:T(8,128)}, u32[]{:S(2)}) copy-start(f32[128,64]{0,1:T(8,128)} %copy-done.2) | copy-start | bytes 98308
  89.1 4.0 %copy-start.7 = (f32[128,64]{0,1:T(8,128)S(1)}, f32[128,64]{0,1:T(8,128)}, u32[]{:S(2)}) copy-start(f32[128,64]{0,1:T(8,128)} %copy-done.6) | copy-start | bytes 98308
  89.2 4.0 %copy-start.8 = (f32[128,63]{0,1:T(8,128)S(1)}, f32[128,63]{0,1:T(8,128)}, u32[]{:S(2)}) copy-start(f32[128,63]{0,1:T(8,128)} %slice.722) | copy-start | bytes 96772
  89.6 5.7 %collective-permute-start.5 = (f32[2,4,4,128]{3,2,1,0:T(4,128)S(1)}, f32[2,4,4,128]{3,2,1,0:T(4,128)S(1)}, u32[]{:S(2)}, u32[]{:S(2)}) collective-permute-start(f32[2,4,4,128]{3,2,1,0:T(4,128)S(1)} %get-tuple-element.47), channel_id=1, source_target_pairs={{1,0},{2,1},{3,2},{4,3},{5,4},{6,5},{7,6},{9,8},{10,9},{11,10},{12... | collective-permute-start | bytes 49160 | tf_op jit(solution)/shard_map/ppermute | solution.py:27
  93.3 3.1 %collective-permute-start.4 = (f32[2,4,4,128]{3,2,1,0:T(4,128)S(1)}, f32[2,4,4,128]{3,2,1,0:T(4,128)S(1)}, u32[]{:S(2)}, u32[]{:S(2)}) collective-permute-start(f32[2,4,4,128]{3,2,1,0:T(4,128)S(1)} %get-tuple-element.46), channel_id=1, source_target_pairs={{0,1},{1,2},{2,3},{3,4},{4,5},{5,6},{6,7},{8,9},{9,10},{10,11},{11... | collective-permute-start | bytes 49160 | tf_op jit(solution)/shard_map/ppermute | solution.py:25
  96.9 7.8 %collective-permute-start.6 = (f32[2,2,4,16,128]{4,3,2,1,0:T(8,128)S(1)}, f32[2,2,4,16,128]{4,3,2,1,0:T(8,128)S(1)}, u32[]{:S(2)}, u32[]{:S(2)}) collective-permute-start(f32[2,2,4,16,128]{4,3,2,1,0:T(8,128)S(1)} %pad_maximum_fusion.11), channel_id=1, source_target_pairs={{8,0},{16,8},{24,16},{32,24},{40,32},{48,40},{56,48},{64,56},{72,6... | collective-permute-start | bytes 393224 | tf_op jit(solution)/shard_map/ppermute | solution.py:27
  98.2 7.5 %collective-permute-start.7 = (f32[2,2,4,16,128]{4,3,2,1,0:T(8,128)S(1)}, f32[2,2,4,16,128]{4,3,2,1,0:T(8,128)S(1)}, u32[]{:S(2)}, u32[]{:S(2)}) collective-permute-start(f32[2,2,4,16,128]{4,3,2,1,0:T(8,128)S(1)} %pad_maximum_fusion.11), channel_id=1, source_target_pairs={{0,8},{8,16},{16,24},{24,32},{32,40},{40,48},{48,56},{56,64},{64,7... | collective-permute-start | bytes 393224 | tf_op jit(solution)/shard_map/ppermute | solution.py:25
  106.4 6.0 %collective-permute-start.9 = (f32[2,2,4,64]{3,2,1,0:T(4,128)S(1)}, f32[2,2,4,64]{3,2,1,0:T(4,128)S(1)}, u32[]{:S(2)}, u32[]{:S(2)}) collective-permute-start(f32[2,2,4,64]{3,2,1,0:T(4,128)S(1)} %get-tuple-element.51), channel_id=1, source_target_pairs={{1,0},{2,1},{3,2},{4,3},{5,4},{6,5},{7,6},{9,8},{10,9},{11,10},{12... | collective-permute-start | bytes 12296 | tf_op jit(solution)/shard_map/ppermute | solution.py:27
  109.4 3.8 %collective-permute-start.8 = (f32[2,2,4,64]{3,2,1,0:T(4,128)S(1)}, f32[2,2,4,64]{3,2,1,0:T(4,128)S(1)}, u32[]{:S(2)}, u32[]{:S(2)}) collective-permute-start(f32[2,2,4,64]{3,2,1,0:T(4,128)S(1)} %get-tuple-element.50), channel_id=1, source_target_pairs={{0,1},{1,2},{2,3},{3,4},{4,5},{5,6},{6,7},{8,9},{9,10},{10,11},{11... | collective-permute-start | bytes 12296 | tf_op jit(solution)/shard_map/ppermute | solution.py:25
  113.6 5.2 %collective-permute-start.10 = (f32[2,2,1,8,64]{4,3,1,0,2:T(8,128)S(1)}, f32[2,2,1,8,64]{4,3,1,0,2:T(8,128)S(1)}, u32[]{:S(2)}, u32[]{:S(2)}) collective-permute-start(f32[2,2,1,8,64]{4,3,1,0,2:T(8,128)S(1)} %maximum_bitcast_fusion.8), channel_id=1, source_target_pairs={{8,0},{16,8},{24,16},{32,24},{40,32},{48,40},{56,48},{64,56},{72,6... | collective-permute-start | bytes 24584 | tf_op jit(solution)/shard_map/ppermute | solution.py:37
  118.8 4.5 %collective-permute-start.11 = (f32[2,2,1,8,64]{4,3,1,0,2:T(8,128)S(1)}, f32[2,2,1,8,64]{4,3,1,0,2:T(8,128)S(1)}, u32[]{:S(2)}, u32[]{:S(2)}) collective-permute-start(f32[2,2,1,8,64]{4,3,1,0,2:T(8,128)S(1)} %bitcast.184), channel_id=1, source_target_pairs={{0,8},{8,16},{16,24},{24,32},{32,40},{40,48},{48,56},{56,64},{64,7... | collective-permute-start | bytes 24584 | tf_op jit(solution)/shard_map/ppermute | solution.py:37
  123.3 5.2 %collective-permute-start.12 = (f32[2,2,1,8,64]{4,3,1,0,2:T(8,128)S(1)}, f32[2,2,1,8,64]{4,3,1,0,2:T(8,128)S(1)}, u32[]{:S(2)}, u32[]{:S(2)}) collective-permute-start(f32[2,2,1,8,64]{4,3,1,0,2:T(8,128)S(1)} %fusion.123), channel_id=1, source_target_pairs={{8,0},{16,8},{24,16},{32,24},{40,32},{48,40},{56,48},{64,56},{72,6... | collective-permute-start | bytes 24584 | tf_op jit(solution)/shard_map/ppermute | solution.py:37
  128.5 6.1 %collective-permute-start.13 = (f32[2,2,1,8,64]{4,3,1,0,2:T(8,128)S(1)}, f32[2,2,1,8,64]{4,3,1,0,2:T(8,128)S(1)}, u32[]{:S(2)}, u32[]{:S(2)}) collective-permute-start(f32[2,2,1,8,64]{4,3,1,0,2:T(8,128)S(1)} %bitcast.194), channel_id=1, source_target_pairs={{0,8},{8,16},{16,24},{24,32},{32,40},{40,48},{48,56},{56,64},{64,7... | collective-permute-start | bytes 24584 | tf_op jit(solution)/shard_map/ppermute | solution.py:37
  135.5 35.7 %all-to-all-start = ((f32[64,1,512]{2,1,0:T(1,128)}), f32[64,1,512]{2,1,0:T(1,128)S(1)}, u32[]{:S(2)}, u32[]{:S(2)}) async-start(f32[64,1,512]{2,1,0:T(1,128)} %reshape.38), calls=%async_computation | async-start | bytes 262144 | tf_op jit(solution)/shard_map/all_to_all | solution.py:48
  173.8 11.8 %collective-permute-start.14 = (f32[2,64,1,32]{1,3,2,0:T(8,128)S(1)}, f32[2,64,1,32]{1,3,2,0:T(8,128)S(1)}, u32[]{:S(2)}, u32[]{:S(2)}) collective-permute-start(f32[2,64,1,32]{1,3,2,0:T(8,128)S(1)} %slice.751), channel_id=1, source_target_pairs={{1,0},{2,1},{3,2},{4,3},{5,4},{6,5},{7,6},{9,8},{10,9},{11,10},{12... | collective-permute-start | bytes 49160 | tf_op jit(solution)/shard_map/ppermute | solution.py:37
  185.6 3.1 %collective-permute-start.15 = (f32[2,64,1,32]{1,3,2,0:T(8,128)S(1)}, f32[2,64,1,32]{1,3,2,0:T(8,128)S(1)}, u32[]{:S(2)}, u32[]{:S(2)}) collective-permute-start(f32[2,64,1,32]{1,3,2,0:T(8,128)S(1)} %slice.753), channel_id=1, source_target_pairs={{0,1},{1,2},{2,3},{3,4},{4,5},{5,6},{6,7},{8,9},{9,10},{10,11},{11... | collective-permute-start | bytes 49160 | tf_op jit(solution)/shard_map/ppermute | solution.py:37
  188.8 5.6 %collective-permute-start.16 = (f32[2,64,1,32]{1,3,2,0:T(8,128)S(1)}, f32[2,64,1,32]{1,3,2,0:T(8,128)S(1)}, u32[]{:S(2)}, u32[]{:S(2)}) collective-permute-start(f32[2,64,1,32]{1,3,2,0:T(8,128)S(1)} %slice.757), channel_id=1, source_target_pairs={{1,0},{2,1},{3,2},{4,3},{5,4},{6,5},{7,6},{9,8},{10,9},{11,10},{12... | collective-permute-start | bytes 49160 | tf_op jit(solution)/shard_map/ppermute | solution.py:37
  194.5 4.2 %collective-permute-start.17 = (f32[2,64,1,32]{1,3,2,0:T(8,128)S(1)}, f32[2,64,1,32]{1,3,2,0:T(8,128)S(1)}, u32[]{:S(2)}, u32[]{:S(2)}) collective-permute-start(f32[2,64,1,32]{1,3,2,0:T(8,128)S(1)} %slice.759), channel_id=1, source_target_pairs={{0,1},{1,2},{2,3},{3,4},{4,5},{5,6},{6,7},{8,9},{9,10},{10,11},{11... | collective-permute-start | bytes 49160 | tf_op jit(solution)/shard_map/ppermute | solution.py:37
where the time goes:
time: 207 us; the launch traced here: 206 us
  starting transfers between devices  82.2 us (40%)
  local copies, waits for them, and re-layouts  66.7 us (32%)
  waiting for transfers between devices  45.1 us (22%)
  other arithmetic  6.59 us (3%)
  matrix products  3.35 us (2%)
  between operations  2.12 us (1%)
    slice x8, local copies, waits for them, and re-layouts, lift_general(): odd_part = lax.slice_in_dim(volume, 1, length, 2, along)  28.9 us
    slice x11, local copies, waits for them, and re-layouts, lift_general(): even_part = lax.slice_in_dim(volume, 0, length, 2, along)  27.4 us
    all_to_all x1, starting transfers between devices, from_everyone(): lax.all_to_all(jnp.broadcast_to(shard[None], (devices, *shard.shape)), ax...  24.5 us
    ppermute x8, starting transfers between devices, shifted(): lax.ppermute(value, axis, [(source, source + steps) for source in range(f...  24 us
    ppermute x8, waiting for transfers between devices, shifted(): lax.ppermute(value, axis, [(source, source + steps) for source in range(f...  19.3 us
    ppermute x5, starting transfers between devices, extended(): lax.ppermute(head, axis, [((i + 1) % count, i) for i in range(ends)])  17.8 us
    ppermute x5, starting transfers between devices, extended(): lax.ppermute(tail, axis, [(i, (i + 1) % count) for i in range(ends)])  15.9 us
    all_to_all x1, waiting for transfers between devices, from_everyone(): lax.all_to_all(jnp.broadcast_to(shard[None], (devices, *shard.shape)), ax...  11.2 us
  transfers between devices with their start and end apart: 19, of which 14 were waited for; matrix products, arithmetic and copies ran while one was open for 7% of the time, Pallas kernels for 0%

commit v1 on v0

v1 whole, which is shorter than its diff:
```python
import jax
import jax.numpy as jnp
import ml_dtypes
import numpy as np
from jax import lax
from jax.experimental import pallas as pl
from jax.experimental.pallas import tpu as pltpu
from jax.sharding import PartitionSpec as P

MESH = pl.DeviceIdType.MESH
F32, BF16 = jnp.float32, jnp.bfloat16

LA = -1.586134342
LB = -0.05298011854
LG = 0.8829110762
LD = 0.4435068522
LZ = 1.149604398
LI = 1.0 / 1.149604398


def lift_matrix(n):
    v = np.eye(n)
    s, d = v[0::2].copy(), v[1::2].copy()

    def nxt(q):
        return np.concatenate([q[1:], q[-1:]])

    def prv(q):
        return np.concatenate([q[:1], q[:-1]])

    d = d + LA * (s + nxt(s))
    s = s + LB * (prv(d) + d)
    d = d + LG * (s + nxt(s))
    s = s + LD * (prv(d) + d)
    return np.concatenate([s * LZ, d * LI])


def chain():
    out, low = {}, np.eye(512)
    for k in (1, 2, 3, 4):
        out[k] = lift_matrix(1024 >> k) @ low
        low = out[k][: 512 >> k]
    return out


CH = chain()
L64 = lift_matrix(64)
H_LOW = [float(L64[16, 32 + k]) for k in range(5)]
H_HIGH = [float(L64[48, 33 + k]) for k in range(4)]


def two(a):
    hi = a.astype(ml_dtypes.bfloat16)
    return hi, (a - hi.astype(np.float64)).astype(ml_dtypes.bfloat16)


def stack_rhs(a):
    hi, lo = two(a)
    return np.concatenate([hi, hi, lo], axis=0)


def stack_lhs(a):
    hi, lo = two(a)
    return np.concatenate([hi, hi, lo], axis=-1)


def y_rows(k, n):
    half, own = 512 >> k, 64 >> k
    return list(range(n * own, (n + 1) * own)) + list(range(half + n * own, half + (n + 1) * own))


def y_block(k, to, cells, rows):
    if not 0 <= to < 8:
        return np.zeros((len(rows), 64))
    return CH[k][[y_rows(k, to)[r] for r in rows]][:, 64 * cells : 64 * cells + 64]


def y_table(k, n):
    own = 64 >> k
    up = list(range(4)) + list(range(own, own + 4))
    down = list(range(2 * own - 4, 2 * own)) + list(range(own - 4, own))
    for to, rows in ((n + 1, up), (n - 1, down)):
        if 0 <= to < 8:
            rest = [r for r in range(2 * own) if r not in rows]
            assert not rest or abs(y_block(k, to, n, rest)).max() < 1e-15
    return np.concatenate(
        [y_block(k, n, n, list(range(2 * own))), y_block(k, n + 1, n, up), y_block(k, n - 1, n, down)]
    )


def y4_table(n):
    rows = np.concatenate([y_block(4, to, n, list(range(8))) for to in (n, n + 1, n - 1)])
    return np.einsum("ry,pq->rpqy", rows, np.eye(8)).reshape(24 * 8, 512)


def tables():
    x4 = CH[4].T
    t = {}
    t["x34"] = stack_rhs(np.concatenate([CH[3].T, x4, x4], axis=1))
    t["x2"] = stack_rhs(CH[2].T)
    t["x1"] = stack_rhs(CH[1].T)
    t["y4"] = np.stack([stack_lhs(y4_table(n)) for n in (0, 3, 7)])
    t["y3"] = np.stack([stack_lhs(y_table(3, n)) for n in range(8)])
    t["y2"] = np.stack([stack_lhs(y_table(2, n)) for n in range(8)])
    low3 = CH[3][:64]
    ca = np.zeros((8, 16, 64))
    fin = np.zeros((64, 128))
    for y in range(8):
        for s in range(15):
            w = 8 * y - 3 + s
            if 0 <= w < 64:
                ca[y, s] = low3[w, 64 * y : 64 * y + 64]
                fin[:, 16 * y + s] = L64[:, w]
        for w in range(64):
            if not 8 * y - 3 <= w <= 8 * y + 11:
                assert abs(low3[w, 64 * y : 64 * y + 64]).max() < 1e-15
    t["ca"] = np.stack([stack_lhs(ca[y]) for y in range(8)])
    t["fin"] = stack_lhs(fin)
    c3 = np.zeros((64, 8, 2, 8), np.float32)
    for w in range(64):
        for i in range(8):
            to = w + i - 3
            if 0 <= to < 64:
                c3[w, i, 0] = CH[3][to, 8 * w : 8 * w + 8]
                c3[w, i, 1] = CH[3][64 + to, 8 * w : 8 * w + 8]
    t["c3"] = c3.reshape(64, 1, 128)
    return t


TAB = tables()
NAMES = ("x34", "y4", "x2", "y3", "y2", "x1", "ca", "fin", "c3")


def halves(x):
    hi = x.astype(BF16)
    return hi, (x - hi.astype(F32)).astype(BF16)


def data_rhs(x):
    hi, lo = halves(x)
    return jnp.concatenate([hi, lo, hi], axis=0)


def dot(a, b):
    return jnp.dot(a, b, preferred_element_type=F32)


def z_states(planes):
    s0, d0, s1 = planes[0], planes[1], planes[2]
    p1 = s0 + LB * (d0 + LA * (s0 + s1))
    sl, dl = planes[-2], planes[-1]
    u1 = dl + LA * sl
    u2 = sl + LB * (planes[-3] + LA * (planes[-4] + sl))
    return (s0, p1), (u1, u2)


def z_lift(planes, p0, p1, u1, u2, first, last, need_high):
    s, d = planes[0::2], planes[1::2]
    m = len(s)
    n0 = jnp.where(last, s[-1], p0)
    d = [d[i] + LA * (s[i] + (s[i + 1] if i + 1 < m else n0)) for i in range(m)]
    before = jnp.where(first, d[0], u1 + LA * s[0])
    s_old = s
    s = [s[i] + LB * ((d[i - 1] if i else before) + d[i]) for i in range(m)]
    n1 = jnp.where(last, s[-1], p1 + LB * d[-1])
    d1 = d
    d = [d[i] + LG * (s[i] + (s[i + 1] if i + 1 < m else n1)) for i in range(m)]
    before2 = jnp.where(first, d[0], before + LG * (u2 + LB * before + s[0]))
    del s_old, d1
    low = [(s[i] + LD * ((d[i - 1] if i else before2) + d[i])) * LZ for i in range(m)]
    return low, [x * LI for x in d] if need_high else None


def main_kernel(v_hbm, x34_h, y4_h, x2_h, y3_h, y2_h, x1_h, ca_h, fin_h, c3_h,
                d1_o, d2_o, d3_o, f_o,
                v, vc, x34, y4, x2, y3, y2, x1, ca, fin, c3,
                so4, ri4, so3, ri3, so2, ri2, t3, t2, ga, gb, st1, zh1, e1, st2, zh2, t2b, st2b, zh2b, s3, r3,
                lsem, ss, rs):
    w, n = lax.axis_index("wide"), lax.axis_index("narrow")
    y, z = w // 8, w % 8
    wfirst, wlast = w == 0, w == 63
    nfirst, nlast = n == 0, n == 7
    n_up, n_dn = (n + 1) % 8, (n + 7) % 8
    w_up, w_dn = (w + 1) % 64, (w + 63) % 64

    loads = [pltpu.make_async_copy(v_hbm, v, lsem.at[0])]
    variant = jnp.minimum(n, 1) + n // 7
    for i, (src, dst) in enumerate(
        (
            (x34_h, x34), (y4_h.at[variant], y4), (x2_h, x2), (y3_h.at[n], y3), (y2_h.at[n], y2),
            (x1_h, x1), (ca_h.at[y], ca), (fin_h, fin), (c3_h.at[w], c3),
        )
    ):
        loads.append(pltpu.make_async_copy(src, dst, lsem.at[1 + i]))
    for c in loads:
        c.start()
    l_v, l_x34, l_y4, l_x2, l_y3, l_y2, l_x1, l_ca, l_fin, l_c3 = loads

    barrier = pltpu.get_barrier_semaphore()
    peers = [(w, n_up), (w, n_dn)]
    peers += [((w + 64 + d) % 64, n) for d in (1, -1, 2, -2, 3, -3, 4, -4)]
    peers += [(y * 8 + (z + d) % 8, n) for d in range(1, 8)]
    peers += [(((y + d) % 8) * 8 + z, n) for d in range(1, 8)]
    for p in peers:
        pl.semaphore_signal(barrier, inc=1, device_id=p, device_id_type=MESH)

    count = [0]
    started = []

    def send(src, dst, to):
        k = count[0]
        count[0] += 1
        c = pltpu.make_async_remote_copy(
            src_ref=src, dst_ref=dst, send_sem=ss.at[k], recv_sem=rs.at[k], device_id=to, device_id_type=MESH
        )
        c.start()
        started.append(c)
        return c

    l_v.wait()
    hi, lo = halves(v[...].reshape(512, 512))
    vc[:, 0:512] = hi
    vc[:, 512:1024] = lo
    vc[:, 1024:1536] = hi
    l_x34.wait()
    xa = dot(vc[...], x34[...])
    l_y4.wait()
    o4 = dot(y4[...], data_rhs(xa[:, 128:256])).reshape(24, 8, 128)
    lane_low = lax.broadcasted_iota(jnp.int32, (8, 128), 1) < 64

    def packed(base):
        return [jnp.where(lane_low, o4[base + r], o4[base + 4 + r]) for r in range(4)]

    own4, up4, dn4 = packed(0), packed(8), packed(16)
    for r in range(4):
        so4[0, r] = up4[r]
        so4[1, r] = dn4[r]

    pl.semaphore_wait(barrier, len(peers))
    a4 = [send(so4.at[0], ri4.at[0], (w, n_up)), send(so4.at[1], ri4.at[1], (w, n_dn))]

    (q0, q1), (q2, q3) = z_states([v[i] for i in range(8)])
    st1[0], st1[1], st1[2], st1[3] = q0, q1, q2, q3
    a1 = [
        send(st1.at[pl.ds(0, 2)], zh1.at[pl.ds(0, 2)], (w_dn, n)),
        send(st1.at[pl.ds(2, 2)], zh1.at[pl.ds(2, 2)], (w_up, n)),
    ]

    l_y3.wait()
    for p in range(8):
        o = dot(y3[...], data_rhs(xa[64 * p : 64 * p + 64, 0:128]))
        t3[p] = o[0:16]
        so3[0, p] = o[16:24]
        so3[1, p] = o[24:32]
    a3 = [send(so3.at[0], ri3.at[0], (w, n_up)), send(so3.at[1], ri3.at[1], (w, n_dn))]
    l_x2.wait()
    l_y2.wait()
    xb = dot(vc[...], x2[...])
    for p in range(8):
        o = dot(y2[...], data_rhs(xb[64 * p : 64 * p + 64]))
        t2[p] = o[0:32]
        so2[0, p] = o[32:40]
        so2[1, p] = o[40:48]
    a2 = [send(so2.at[0], ri2.at[0], (w, n_up)), send(so2.at[1], ri2.at[1], (w, n_dn))]

    for c in a4:
        c.wait_recv()
    here = pl.ds(pl.multiple_of(z * 8, 8), 8)
    for r in range(4):
        add = jnp.where(nfirst, 0.0, ri4[0, r]) + jnp.where(nlast, 0.0, ri4[1, r])
        ga[r, here, :] = own4[r] + add
    ga_sends = [
        send(ga.at[:, here, :], ga.at[:, here, :], (y * 8 + (z + d) % 8, n)) for d in (4, 3, 5, 2, 6, 1, 7)
    ]

    def add_parts(t, ri, own):
        width = t.shape[-1]
        sub_low = lax.broadcasted_iota(jnp.int32, (8, width), 0) < 4
        for p in range(8):
            up = jnp.where(nfirst, 0.0, ri[0, p])
            dn = jnp.where(nlast, 0.0, ri[1, p])
            up_r, dn_r = pltpu.roll(up, 4, 0), pltpu.roll(dn, 4, 0)
            t[p, 0:8] = t[p, 0:8] + jnp.where(sub_low, up, 0.0)
            t[p, own : own + 8] = t[p, own : own + 8] + jnp.where(sub_low, up_r, 0.0)
            t[p, own - 8 : own] = t[p, own - 8 : own] + jnp.where(sub_low, 0.0, dn)
            t[p, 2 * own - 8 : 2 * own] = t[p, 2 * own - 8 : 2 * own] + jnp.where(sub_low, 0.0, dn_r)

    for c in a2:
        c.wait_recv()
    add_parts(t2, ri2, 16)
    (q0, q1), (q2, q3) = z_states([t2[i] for i in range(8)])
    st2[0], st2[1], st2[2], st2[3] = q0, q1, q2, q3
    b2 = [
        send(st2.at[pl.ds(0, 2)], zh2.at[pl.ds(0, 2)], (w_dn, n)),
        send(st2.at[pl.ds(2, 2)], zh2.at[pl.ds(2, 2)], (w_up, n)),
    ]

    for c in a3:
        c.wait_recv()
    add_parts(t3, ri3, 8)
    l_c3.wait()
    planes3 = [t3[p] for p in range(8)]
    b3 = []
    for i in (7, 6, 5, 4, 2, 1, 0, 3):
        for j in range(2):
            acc = planes3[0] * c3[0, i * 16 + j * 8]
            for p in range(1, 8):
                acc = acc + planes3[p] * c3[0, i * 16 + j * 8 + p]
            s3[i, j] = acc
        if i != 3:
            b3.append(send(s3.at[i], r3.at[i], ((w + 64 + i - 3) % 64, n)))

    l_ca.wait()
    for c in ga_sends:
        c.wait_recv()
    cat = jnp.concatenate([ga[r] for r in range(4)], axis=1)
    part = dot(ca[...], data_rhs(cat))
    for r in range(4):
        gb[y, r] = part[:, 128 * r : 128 * r + 128]
    gb_sends = [send(gb.at[y], gb.at[y], (((y + d) % 8) * 8 + z, n)) for d in (4, 3, 5, 2, 6, 1, 7)]

    for c in b2:
        c.wait_recv()
    low, _ = z_lift([t2[i] for i in range(8)], zh2[0], zh2[1], zh2[2], zh2[3], wfirst, wlast, False)
    (q0, q1), (q2, q3) = z_states(low)
    for i in range(4):
        t2b[i] = low[i]
    st2b[0], st2b[1], st2b[2], st2b[3] = q0, q1, q2, q3
    c2 = [
        send(st2b.at[pl.ds(0, 2)], zh2b.at[pl.ds(0, 2)], (w_dn, n)),
        send(st2b.at[pl.ds(2, 2)], zh2b.at[pl.ds(2, 2)], (w_up, n)),
    ]

    for c in a1:
        c.wait_recv()
    for q in range(8):
        rows = slice(8 * q, 8 * q + 8)
        low, high = z_lift(
            [v[i, rows] for i in range(8)], zh1[0, rows], zh1[1, rows], zh1[2, rows], zh1[3, rows], wfirst, wlast, True
        )
        for i in range(4):
            v[i, rows] = low[i]
            v[4 + i, rows] = high[i]
    hi, lo = halves(v[...].reshape(512, 512))
    vc[:, 0:512] = hi
    vc[:, 512:1024] = lo
    vc[:, 1024:1536] = hi
    l_x1.wait()
    for h in range(2):
        o = dot(vc[...], x1[:, 256 * h : 256 * h + 256]).reshape(8, 64, 256)
        for q in range(2):
            e1[2 * h + q, :, 8:72, :] = o[:, :, 128 * q : 128 * q + 128]
    c1 = [
        send(e1.at[:, :, pl.ds(64, 8), :], e1.at[:, :, pl.ds(0, 8), :], (w, n_up)),
        send(e1.at[:, :, pl.ds(8, 8), :], e1.at[:, :, pl.ds(72, 8), :], (w, n_dn)),
    ]

    for c in b3:
        c.wait_recv()
    for j in range(2):
        acc = s3[3, j]
        for i in range(8):
            if i != 3:
                src = w - (i - 3)
                acc = acc + jnp.where((src >= 0) & (src < 64), r3[i, j], 0.0)
        for b in range(4):
            band = 4 * j + b
            if band:
                rows = slice(8 * (b // 2), 8 * (b // 2) + 8)
                cols = slice(64 * (b % 2), 64 * (b % 2) + 64)
                d3_o[band - 1, 0] = acc[rows, cols]

    for c in c2:
        c.wait_recv()
    low, high = z_lift([t2b[i] for i in range(4)], zh2b[0], zh2b[1], zh2b[2], zh2b[3], wfirst, wlast, True)
    for band in range(1, 8):
        src = high if band >= 4 else low
        by, bx = (band // 2) % 2, band % 2
        for i in range(2):
            d2_o[band - 1, i] = src[i][16 * by : 16 * by + 16, 128 * bx : 128 * bx + 128]

    for c in c1:
        c.wait_recv()

    @pl.when(nfirst)
    def _():
        for k in range(1, 5):
            e1[:, :, 8 - k : 9 - k, :] = e1[:, :, 8 + k : 9 + k, :]

    @pl.when(nlast)
    def _():
        for k in range(1, 5):
            e1[:, :, 71 + k : 72 + k, :] = e1[:, :, 71 - k : 72 - k, :]

    def tap(c, i, off):
        return e1[c, i, pl.ds(8 + off, 32, stride=2), :]

    for i in range(8):
        bz, zz = i // 4, i % 4
        for c in range(4):
            bx, cols = c // 2, slice(128 * (c % 2), 128 * (c % 2) + 128)
            if bz or bx:
                low = H_LOW[0] * tap(c, i, 0)
                for k in range(1, 5):
                    low = low + H_LOW[k] * (tap(c, i, -k) + tap(c, i, k))
                d1_o[4 * bz + bx - 1, zz, :, cols] = low
            high = H_HIGH[0] * tap(c, i, 1)
            for k in range(1, 4):
                high = high + H_HIGH[k] * (tap(c, i, 1 - k) + tap(c, i, 1 + k))
            d1_o[4 * bz + 2 + bx - 1, zz, :, cols] = high

    l_fin.wait()
    for c in gb_sends:
        c.wait_recv()
    cat = jnp.concatenate([gb[:, r].reshape(128, 128) for r in range(4)], axis=1)
    f_o[...] = dot(fin[...], data_rhs(cat))

    for c in started:
        c.wait_send()


def write_kernel(d1, d2, d3, f, o1, o2, o3, o4, buf, sem):
    copies = [pltpu.make_async_copy(a, b, sem.at[i]) for i, (a, b) in enumerate(((d1, o1), (d2, o2), (d3, o3)))]
    for c in copies:
        c.start()
    for bz in range(2):
        for r in range(4):
            tile = f[32 * bz : 32 * bz + 32, 128 * r : 128 * r + 128]
            for b in range(4):
                buf[4 * bz + b, :, r, :] = tile[:, 32 * b : 32 * b + 32]
    last = pltpu.make_async_copy(buf, o4, sem.at[3])
    last.start()
    for c in copies + [last]:
        c.wait()


VM, ANY = pl.BlockSpec(memory_space=pltpu.VMEM), pl.BlockSpec(memory_space=pl.ANY)
OUTS = ((7, 4, 32, 256), (7, 2, 16, 128), (7, 1, 8, 64), (8, 32, 4, 32))


def per_device(pressure):
    tabs = [jnp.asarray(TAB[k]) for k in NAMES]
    vm = lambda *s: pltpu.VMEM(s, F32)
    vb = lambda *s: pltpu.VMEM(s, BF16)
    sems = 64
    mids = OUTS[:3] + ((64, 512),)
    mid = pl.pallas_call(
        main_kernel,
        out_shape=[jax.ShapeDtypeStruct(s, F32) for s in mids],
        in_specs=[ANY] * 10,
        out_specs=[VM] * 4,
        scratch_shapes=[
            vm(8, 64, 512), vb(512, 1536),
            vb(1536, 256), vb(192, 1536), vb(1536, 256), vb(32, 192), vb(48, 192), vb(1536, 512),
            vb(16, 192), vb(64, 384), pltpu.SMEM((1, 128), F32),
            vm(2, 4, 8, 128), vm(2, 4, 8, 128), vm(2, 8, 8, 128), vm(2, 8, 8, 128), vm(2, 8, 8, 256), vm(2, 8, 8, 256),
            vm(8, 16, 128), vm(8, 32, 256), vm(4, 64, 128), vm(8, 4, 16, 128),
            vm(4, 64, 512), vm(4, 64, 512), vm(4, 8, 80, 128),
            vm(4, 32, 256), vm(4, 32, 256), vm(4, 32, 256), vm(4, 32, 256), vm(4, 32, 256),
            vm(8, 2, 16, 128), vm(8, 2, 16, 128),
            pltpu.SemaphoreType.DMA((10,)), pltpu.SemaphoreType.DMA((sems,)), pltpu.SemaphoreType.DMA((sems,)),
        ],
        compiler_params=pltpu.CompilerParams(
            collective_id=0, has_side_effects=True, vmem_limit_bytes=48 * 1024 * 1024
        ),
        name="exchange",
    )(pressure, *tabs)
    return tuple(
        pl.pallas_call(
            write_kernel,
            out_shape=[jax.ShapeDtypeStruct(s, F32) for s in OUTS],
            in_specs=[VM] * 4,
            out_specs=[ANY] * 4,
            scratch_shapes=[pltpu.VMEM(OUTS[3], F32), pltpu.SemaphoreType.DMA((4,))],
            compiler_params=pltpu.CompilerParams(vmem_limit_bytes=16 * 1024 * 1024),
            name="write",
        )(*mid)
    )


def solution(mesh):
    return jax.shard_map(
        per_device,
        mesh=mesh,
        in_specs=(P("wide", "narrow", None),),
        out_specs=(
            P(None, "wide", "narrow", None),
            P(None, "wide", "narrow", None),
            P(None, "wide", "narrow", None),
            P(None, None, "narrow", None),
        ),
        check_vma=False,
    )
```

time: 207 us -> 54.1 us (0.26)
  starting transfers between devices: 82.2 us -> 0 us
  local copies, waits for them, and re-layouts: 66.7 us -> 9.12 us
  waiting for transfers between devices: 45.1 us -> 0 us
  Pallas kernels: 0 us -> 43.8 us
  other arithmetic: 6.59 us -> 0 us
  matrix products: 3.35 us -> 0 us
    slice x93 -> x0, local copies, waits for them, and re-layouts: 62.8 us -> none  [the longest x8 28.9 us: lift_general(): odd_part = lax.slice_in_dim(volume, 1, length, 2, along)]
    ppermute x18 -> x0, starting transfers between devices: 57.7 us -> none  [the longest x8 24 us: shifted(): lax.ppermute(value, axis, [(source, source + steps) for source in range(f...]
    pallas_call x0 -> x2, Pallas kernels: none -> 43.8 us  [the longest x1 41.9 us: per_device(): pl.pallas_call(main_kernel, out_shape=[jax.ShapeDtypeStruct(s, F32) for s...]
    ppermute x18 -> x0, waiting for transfers between devices: 33.8 us -> none  [the longest x8 19.3 us: shifted(): lax.ppermute(value, axis, [(source, source + steps) for source in range(f...]
    all_to_all x1 -> x0, starting transfers between devices: 24.5 us -> none  [from_everyone(): lax.all_to_all(jnp.broadcast_to(shard[None], (devices, *shard.shape)), ax...]
    all_to_all x1 -> x0, waiting for transfers between devices: 11.2 us -> none  [from_everyone(): lax.all_to_all(jnp.broadcast_to(shard[None], (devices, *shard.shape)), ax...]
    unnamed x21 -> x18, local copies, waits for them, and re-layouts: 2.99 us -> 9.12 us
    dot_general x4 -> x0, matrix products: 3.35 us -> none  [lift_columns(): jnp.einsum('zyi,bij->bzyj', volume, lift_table, precision=lax.Precision.H...]
  transfers between devices with their start and end apart: 19 -> 0, of which waited for: 14 -> 0; matrix products, arithmetic and copies ran while one was open for 7% -> 0% of each run, Pallas kernels for 0% -> 0%
where the time goes in v1:
time: 54.1 us; the launch traced here: 53.6 us
  Pallas kernels  43.8 us (81%)
  local copies, waits for them, and re-layouts  9.12 us (17%)
  between operations  0.65 us (1%)
    pallas_call x1, Pallas kernels, per_device(): pl.pallas_call(main_kernel, out_shape=[jax.ShapeDtypeStruct(s, F32) for s...  41.9 us
    unnamed x18, local copies, waits for them, and re-layouts  9.12 us
    pallas_call x1, Pallas kernels, per_device(): pl.pallas_call(write_kernel, out_shape=[jax.ShapeDtypeStruct(s, F32) for...  1.96 us

profile of v1, /device:TPU:1, one launch (start us, length us, event | category | flops | bytes accessed | tf_op | source)
XLA Modules:
  0.0 53.6 jit_solution(2249727266521724994)
XLA Ops:
  0.6 0.0 copy-start
  0.6 1.4 %copy-done = bf16[1536,512]{1,0:T(8,128)(2,1)S(1)} copy-done((bf16[1536,512]{1,0:T(8,128)(2,1)S(1)}, bf16[1536,512]{1,0:T(8,128)(2,1)}, u32[]{:S(2)}) %copy-start) | copy-done | bytes 1572888
  2.0 0.0 copy-start.1
  2.0 1.2 %copy-done.1 = f32[8,64,512]{2,1,0:T(8,128)S(1)} copy-done((f32[8,64,512]{2,1,0:T(8,128)S(1)}, f32[8,64,512]{2,1,0:T(8,128)}, u32[]{:S(2)}) %copy-start.1) | copy-done | bytes 1048600
  3.3 0.0 copy-start.2
  3.3 1.1 %copy-done.2 = bf16[1536,256]{1,0:T(8,128)(2,1)S(1)} copy-done((bf16[1536,256]{1,0:T(8,128)(2,1)S(1)}, bf16[1536,256]{1,0:T(8,128)(2,1)}, u32[]{:S(2)}) %copy-start.2) | copy-done | bytes 786456
  4.4 0.0 copy-start.3
  4.4 1.1 %copy-done.3 = bf16[1536,256]{1,0:T(8,128)(2,1)S(1)} copy-done((bf16[1536,256]{1,0:T(8,128)(2,1)S(1)}, bf16[1536,256]{1,0:T(8,128)(2,1)}, u32[]{:S(2)}) %copy-start.3) | copy-done | bytes 786456
  5.5 0.0 copy-start.4
  5.5 0.9 %copy-done.4 = bf16[8,48,192]{2,1,0:T(8,128)(2,1)S(1)} copy-done((bf16[8,48,192]{2,1,0:T(8,128)(2,1)S(1)}, bf16[8,48,192]{2,1,0:T(8,128)(2,1)}, u32[]{:S(2)}) %copy-start.4) | copy-done | bytes 147480
  6.5 0.0 copy-start.5
  6.5 0.9 %copy-done.5 = bf16[8,32,192]{2,1,0:T(8,128)(2,1)S(1)} copy-done((bf16[8,32,192]{2,1,0:T(8,128)(2,1)S(1)}, bf16[8,32,192]{2,1,0:T(8,128)(2,1)}, u32[]{:S(2)}) %copy-start.5) | copy-done | bytes 98328
  7.4 0.0 copy-start.6
  7.4 0.8 %copy-done.6 = bf16[8,16,192]{2,1,0:T(8,128)(2,1)S(1)} copy-done((bf16[8,16,192]{2,1,0:T(8,128)(2,1)S(1)}, bf16[8,16,192]{2,1,0:T(8,128)(2,1)}, u32[]{:S(2)}) %copy-start.6) | copy-done | bytes 49176
  8.2 0.0 copy-start.7
  8.2 0.8 %copy-done.7 = bf16[64,384]{1,0:T(8,128)(2,1)S(1)} copy-done((bf16[64,384]{1,0:T(8,128)(2,1)S(1)}, bf16[64,384]{1,0:T(8,128)(2,1)}, u32[]{:S(2)}) %copy-start.7) | copy-done | bytes 49176
  9.0 0.0 copy-start.8
  9.0 0.8 %copy-done.8 = f32[64,1,128]{2,1,0:T(1,128)S(1)} copy-done((f32[64,1,128]{2,1,0:T(1,128)S(1)}, f32[64,1,128]{2,1,0:T(1,128)}, u32[]{:S(2)}) %copy-start.8) | copy-done | bytes 32792
  9.8 41.9 %exchange.1 = (f32[7,4,32,256]{3,2,1,0:T(8,128)S(1)}, f32[7,2,16,128]{3,2,1,0:T(8,128)S(1)}, f32[7,1,8,64]{3,2,1,0:T(8,128)S(1)}, f32[64,512]{1,0:T(8,128)S(1)}) custom-call(f32[8,64,512]{2,1,0:T(8,128)S(1)} %copy-done.1, bf16[1536,256]{1,0:T(8,128)(2,1)S(1)} %copy-done.3, bf16[3,192,1536]{2,1,0:T(8,128)(2,1)} %constant.19.clone.y4_h, ...), custom_call_target="tpu_custom_call" | custom-call | tf_op jit(solution)/shard_map/exchange/pallas_call | solution.py:447
  51.7 2.0 %write.1 = (f32[7,4,32,256]{3,2,1,0:T(8,128)}, f32[7,2,16,128]{3,2,1,0:T(8,128)}, f32[7,1,8,64]{3,2,1,0:T(8,128)}, f32[8,32,4,32]{3,2,1,0:T(4,128)}) custom-call(f32[7,4,32,256]{3,2,1,0:T(8,128)S(1)} %get-tuple-element.8.d1, f32[7,2,16,128]{3,2,1,0:T(8,128)S(1)} %get-tuple-element.9.d2, f32[7,1,8,64]{3,2,1,0:T(8,128)S(1)} %get-tuple-element.10.d3, ...), custom_call_target="tpu_custom_call" | custom-call | tf_op jit(solution)/shard_map/write/pallas_call | solution.py:469
Async XLA Ops:
  0.6 1.4 %copy-start = (bf16[1536,512]{1,0:T(8,128)(2,1)S(1)}, bf16[1536,512]{1,0:T(8,128)(2,1)}, u32[]{:S(2)}) copy-start(bf16[1536,512]{1,0:T(8,128)(2,1)} %constant.23.clone.x1_h) | copy-start | bytes 4718596
  2.0 1.2 %copy-start.1 = (f32[8,64,512]{2,1,0:T(8,128)S(1)}, f32[8,64,512]{2,1,0:T(8,128)}, u32[]{:S(2)}) copy-start(f32[8,64,512]{2,1,0:T(8,128)} %v_hbm.1) | copy-start | bytes 3145732
  3.3 1.1 %copy-start.2 = (bf16[1536,256]{1,0:T(8,128)(2,1)S(1)}, bf16[1536,256]{1,0:T(8,128)(2,1)}, u32[]{:S(2)}) copy-start(bf16[1536,256]{1,0:T(8,128)(2,1)} %constant.20.clone.x2_h) | copy-start | bytes 2359300
  4.4 1.1 %copy-start.3 = (bf16[1536,256]{1,0:T(8,128)(2,1)S(1)}, bf16[1536,256]{1,0:T(8,128)(2,1)}, u32[]{:S(2)}) copy-start(bf16[1536,256]{1,0:T(8,128)(2,1)} %constant.18.clone.x34_h) | copy-start | bytes 2359300
  5.5 0.9 %copy-start.4 = (bf16[8,48,192]{2,1,0:T(8,128)(2,1)S(1)}, bf16[8,48,192]{2,1,0:T(8,128)(2,1)}, u32[]{:S(2)}) copy-start(bf16[8,48,192]{2,1,0:T(8,128)(2,1)} %constant.22.clone.y2_h) | copy-start | bytes 442372
  6.5 0.9 %copy-start.5 = (bf16[8,32,192]{2,1,0:T(8,128)(2,1)S(1)}, bf16[8,32,192]{2,1,0:T(8,128)(2,1)}, u32[]{:S(2)}) copy-start(bf16[8,32,192]{2,1,0:T(8,128)(2,1)} %constant.21.clone.y3_h) | copy-start | bytes 294916
  7.4 0.8 %copy-start.6 = (bf16[8,16,192]{2,1,0:T(8,128)(2,1)S(1)}, bf16[8,16,192]{2,1,0:T(8,128)(2,1)}, u32[]{:S(2)}) copy-start(bf16[8,16,192]{2,1,0:T(8,128)(2,1)} %constant.24.clone.ca_h) | copy-start | bytes 147460
  8.2 0.8 %copy-start.7 = (bf16[64,384]{1,0:T(8,128)(2,1)S(1)}, bf16[64,384]{1,0:T(8,128)(2,1)}, u32[]{:S(2)}) copy-start(bf16[64,384]{1,0:T(8,128)(2,1)} %constant.25.clone.fin_h) | copy-start | bytes 147460
  9.0 0.8 %copy-start.8 = (f32[64,1,128]{2,1,0:T(1,128)S(1)}, f32[64,1,128]{2,1,0:T(1,128)}, u32[]{:S(2)}) copy-start(f32[64,1,128]{2,1,0:T(1,128)} %constant.26.clone.c3_h) | copy-start | bytes 98308

commit v2 on v1

--- a/solution.py
+++ b/solution.py
@@ -116,19 +116,40 @@
                 assert abs(low3[w, 64 * y : 64 * y + 64]).max() < 1e-15
     t["ca"] = np.stack([stack_lhs(ca[y]) for y in range(8)])
     t["fin"] = stack_lhs(fin)
-    c3 = np.zeros((64, 8, 2, 8), np.float32)
+    c3 = np.zeros((64, 8, 2, 8))
     for w in range(64):
         for i in range(8):
             to = w + i - 3
             if 0 <= to < 64:
                 c3[w, i, 0] = CH[3][to, 8 * w : 8 * w + 8]
                 c3[w, i, 1] = CH[3][64 + to, 8 * w : 8 * w + 8]
-    t["c3"] = c3.reshape(64, 1, 128)
+    for w in range(4, 60):
+        assert abs(c3[w] - c3[30]).max() < 1e-15
+    c3 = c3[[0, 1, 2, 3, 30, 60, 61, 62, 63]].reshape(9, 128, 1)
+    t["c3"] = np.concatenate([np.repeat(h, 128, axis=2) for h in two(c3)], axis=2)
     return t
 
 
-TAB = tables()
-NAMES = ("x34", "y4", "x2", "y3", "y2", "x1", "ca", "fin", "c3")
+def pack(t):
+    blocks = {
+        "x1": t["x1"],
+        "xs": np.concatenate([t["x34"], t["x2"]], axis=1),
+        "y4": t["y4"].reshape(3, 192, 3, 512).transpose(0, 2, 1, 3).reshape(-1, 512),
+        "y2": t["y2"].reshape(-1, 192),
+        "y3": t["y3"].reshape(-1, 192),
+        "ca": t["ca"].reshape(-1, 192),
+        "fin": t["fin"],
+        "c3": t["c3"].reshape(-1, 256),
+    }
+    at, row, rows = {}, 0, []
+    for name, block in blocks.items():
+        at[name] = row
+        row += block.shape[0]
+        rows.append(np.pad(block, ((0, 0), (0, 512 - block.shape[1]))))
+    return np.concatenate(rows, axis=0), at
+
+
+TAB, AT = pack(tables())
 
 
 def halves(x):
@@ -171,9 +192,9 @@
     return low, [x * LI for x in d] if need_high else None
 
 
-def main_kernel(v_hbm, x34_h, y4_h, x2_h, y3_h, y2_h, x1_h, ca_h, fin_h, c3_h,
+def main_kernel(v_hbm, tab,
                 d1_o, d2_o, d3_o, f_o,
-                v, vc, x34, y4, x2, y3, y2, x1, ca, fin, c3,
+                v, vc, x34, y4, x2, y3, y2, x1, ca, fin, c3b, c3,
                 so4, ri4, so3, ri3, so2, ri2, t3, t2, ga, gb, st1, zh1, e1, st2, zh2, t2b, st2b, zh2b, s3, r3,
                 lsem, ss, rs):
     w, n = lax.axis_index("wide"), lax.axis_index("narrow")
@@ -184,17 +205,29 @@
     w_up, w_dn = (w + 1) % 64, (w + 63) % 64
 
     loads = [pltpu.make_async_copy(v_hbm, v, lsem.at[0])]
-    variant = jnp.minimum(n, 1) + n // 7
-    for i, (src, dst) in enumerate(
-        (
-            (x34_h, x34), (y4_h.at[variant], y4), (x2_h, x2), (y3_h.at[n], y3), (y2_h.at[n], y2),
-            (x1_h, x1), (ca_h.at[y], ca), (fin_h, fin), (c3_h.at[w], c3),
-        )
-    ):
-        loads.append(pltpu.make_async_copy(src, dst, lsem.at[1 + i]))
+
+    def load(name, index, dst, lane=0):
+        rows, lanes = dst.shape
+        first = AT[name] + index * rows
+        if not isinstance(first, int):
+            first = pl.multiple_of(first, 16)
+        src = tab.at[pl.ds(first, rows), pl.ds(lane, lanes)]
+        c = pltpu.make_async_copy(src, dst, lsem.at[len(loads)])
+        loads.append(c)
+        return c
+
+    l_v = loads[0]
+    l_x34 = load("xs", 0, x34)
+    l_y4 = load("y4", jnp.minimum(n, 1) + n // 7, y4)
+    l_x2 = load("xs", 0, x2, 256)
+    l_y3 = load("y3", n, y3)
+    l_y2 = load("y2", n, y2)
+    l_c3 = load("c3", jnp.minimum(w, 4) + jnp.maximum(w - 59, 0), c3b)
+    l_ca = load("ca", y, ca)
+    l_x1 = load("x1", 0, x1)
+    l_fin = load("fin", 0, fin)
     for c in loads:
         c.start()
-    l_v, l_x34, l_y4, l_x2, l_y3, l_y2, l_x1, l_ca, l_fin, l_c3 = loads
 
     barrier = pltpu.get_barrier_semaphore()
     peers = [(w, n_up), (w, n_dn)]
@@ -225,7 +258,9 @@
     l_x34.wait()
     xa = dot(vc[...], x34[...])
     l_y4.wait()
-    o4 = dot(y4[...], data_rhs(xa[:, 128:256])).reshape(24, 8, 128)
+    hi, lo = halves(xa[:, 128:256])
+    o4 = dot(y4[0:192], hi) + dot(y4[192:384], lo) + dot(y4[384:576], hi)
+    o4 = o4.reshape(24, 8, 128)
     lane_low = lax.broadcasted_iota(jnp.int32, (8, 128), 1) < 64
 
     def packed(base):
@@ -248,7 +283,7 @@
 
     l_y3.wait()
     for p in range(8):
-        o = dot(y3[...], data_rhs(xa[64 * p : 64 * p + 64, 0:128]))
+        o = dot(y3[:, 0:192], data_rhs(xa[64 * p : 64 * p + 64, 0:128]))
         t3[p] = o[0:16]
         so3[0, p] = o[16:24]
         so3[1, p] = o[24:32]
@@ -257,7 +292,7 @@
     l_y2.wait()
     xb = dot(vc[...], x2[...])
     for p in range(8):
-        o = dot(y2[...], data_rhs(xb[64 * p : 64 * p + 64]))
+        o = dot(y2[:, 0:192], data_rhs(xb[64 * p : 64 * p + 64]))
         t2[p] = o[0:32]
         so2[0, p] = o[32:40]
         so2[1, p] = o[40:48]
@@ -295,41 +330,14 @@
         send(st2.at[pl.ds(2, 2)], zh2.at[pl.ds(2, 2)], (w_up, n)),
     ]
 
-    for c in a3:
-        c.wait_recv()
-    add_parts(t3, ri3, 8)
-    l_c3.wait()
-    planes3 = [t3[p] for p in range(8)]
-    b3 = []
-    for i in (7, 6, 5, 4, 2, 1, 0, 3):
-        for j in range(2):
-            acc = planes3[0] * c3[0, i * 16 + j * 8]
-            for p in range(1, 8):
-                acc = acc + planes3[p] * c3[0, i * 16 + j * 8 + p]
-            s3[i, j] = acc
-        if i != 3:
-            b3.append(send(s3.at[i], r3.at[i], ((w + 64 + i - 3) % 64, n)))
-
     l_ca.wait()
     for c in ga_sends:
         c.wait_recv()
     cat = jnp.concatenate([ga[r] for r in range(4)], axis=1)
-    part = dot(ca[...], data_rhs(cat))
+    part = dot(ca[:, 0:192], data_rhs(cat))
     for r in range(4):
         gb[y, r] = part[:, 128 * r : 128 * r + 128]
     gb_sends = [send(gb.at[y], gb.at[y], (((y + d) % 8) * 8 + z, n)) for d in (4, 3, 5, 2, 6, 1, 7)]
-
-    for c in b2:
-        c.wait_recv()
-    low, _ = z_lift([t2[i] for i in range(8)], zh2[0], zh2[1], zh2[2], zh2[3], wfirst, wlast, False)
-    (q0, q1), (q2, q3) = z_states(low)
-    for i in range(4):
-        t2b[i] = low[i]
-    st2b[0], st2b[1], st2b[2], st2b[3] = q0, q1, q2, q3
-    c2 = [
-        send(st2b.at[pl.ds(0, 2)], zh2b.at[pl.ds(0, 2)], (w_dn, n)),
-        send(st2b.at[pl.ds(2, 2)], zh2b.at[pl.ds(2, 2)], (w_up, n)),
-    ]
 
     for c in a1:
         c.wait_recv()
@@ -355,29 +363,34 @@
         send(e1.at[:, :, pl.ds(8, 8), :], e1.at[:, :, pl.ds(72, 8), :], (w, n_dn)),
     ]
 
-    for c in b3:
-        c.wait_recv()
-    for j in range(2):
-        acc = s3[3, j]
-        for i in range(8):
-            if i != 3:
-                src = w - (i - 3)
-                acc = acc + jnp.where((src >= 0) & (src < 64), r3[i, j], 0.0)
-        for b in range(4):
-            band = 4 * j + b
-            if band:
-                rows = slice(8 * (b // 2), 8 * (b // 2) + 8)
-                cols = slice(64 * (b % 2), 64 * (b % 2) + 64)
-                d3_o[band - 1, 0] = acc[rows, cols]
-
-    for c in c2:
-        c.wait_recv()
-    low, high = z_lift([t2b[i] for i in range(4)], zh2b[0], zh2b[1], zh2b[2], zh2b[3], wfirst, wlast, True)
-    for band in range(1, 8):
-        src = high if band >= 4 else low
-        by, bx = (band // 2) % 2, band % 2
-        for i in range(2):
-            d2_o[band - 1, i] = src[i][16 * by : 16 * by + 16, 128 * bx : 128 * bx + 128]
+    for c in b2:
+        c.wait_recv()
+    low, _ = z_lift([t2[i] for i in range(8)], zh2[0], zh2[1], zh2[2], zh2[3], wfirst, wlast, False)
+    (q0, q1), (q2, q3) = z_states(low)
+    for i in range(4):
+        t2b[i] = low[i]
+    st2b[0], st2b[1], st2b[2], st2b[3] = q0, q1, q2, q3
+    c2 = [
+        send(st2b.at[pl.ds(0, 2)], zh2b.at[pl.ds(0, 2)], (w_dn, n)),
+        send(st2b.at[pl.ds(2, 2)], zh2b.at[pl.ds(2, 2)], (w_up, n)),
+    ]
+
+    for c in a3:
+        c.wait_recv()
+    add_parts(t3, ri3, 8)
+    l_c3.wait()
+    c3[...] = c3b[:, 0:128].astype(F32) + c3b[:, 128:256].astype(F32)
+    planes3 = [t3[p] for p in range(8)]
+    b3 = []
+    for i in (7, 6, 5, 4, 2, 1, 0, 3):
+        for j in range(2):
+            k = i * 16 + j * 8
+            acc = planes3[0] * c3[k : k + 1]
+            for p in range(1, 8):
+                acc = acc + planes3[p] * c3[k + p : k + p + 1]
+            s3[i, j] = acc
+        if i != 3:
+            b3.append(send(s3.at[i], r3.at[i], ((w + 64 + i - 3) % 64, n)))
 
     for c in c1:
         c.wait_recv()
@@ -409,6 +422,30 @@
                 high = high + H_HIGH[k] * (tap(c, i, 1 - k) + tap(c, i, 1 + k))
             d1_o[4 * bz + 2 + bx - 1, zz, :, cols] = high
 
+    for c in b3:
+        c.wait_recv()
+    for j in range(2):
+        acc = s3[3, j]
+        for i in range(8):
+            if i != 3:
+                src = w - (i - 3)
+                acc = acc + jnp.where((src >= 0) & (src < 64), r3[i, j], 0.0)
+        for b in range(4):
+            band = 4 * j + b
+            if band:
+                rows = slice(8 * (b // 2), 8 * (b // 2) + 8)
+                cols = slice(64 * (b % 2), 64 * (b % 2) + 64)
+                d3_o[band - 1, 0] = acc[rows, cols]
+
+    for c in c2:
+        c.wait_recv()
+    low, high = z_lift([t2b[i] for i in range(4)], zh2b[0], zh2b[1], zh2b[2], zh2b[3], wfirst, wlast, True)
+    for band in range(1, 8):
+        src = high if band >= 4 else low
+        by, bx = (band // 2) % 2, band % 2
+        for i in range(2):
+            d2_o[band - 1, i] = src[i][16 * by : 16 * by + 16, 128 * bx : 128 * bx + 128]
+
     l_fin.wait()
     for c in gb_sends:
         c.wait_recv()
@@ -439,7 +476,6 @@
 
 
 def per_device(pressure):
-    tabs = [jnp.asarray(TAB[k]) for k in NAMES]
     vm = lambda *s: pltpu.VMEM(s, F32)
     vb = lambda *s: pltpu.VMEM(s, BF16)
     sems = 64
@@ -447,12 +483,12 @@
     mid = pl.pallas_call(
         main_kernel,
         out_shape=[jax.ShapeDtypeStruct(s, F32) for s in mids],
-        in_specs=[ANY] * 10,
+        in_specs=[ANY] * 2,
         out_specs=[VM] * 4,
         scratch_shapes=[
             vm(8, 64, 512), vb(512, 1536),
-            vb(1536, 256), vb(192, 1536), vb(1536, 256), vb(32, 192), vb(48, 192), vb(1536, 512),
-            vb(16, 192), vb(64, 384), pltpu.SMEM((1, 128), F32),
+            vb(1536, 256), vb(576, 512), vb(1536, 256), vb(32, 256), vb(48, 256), vb(1536, 512),
+            vb(16, 256), vb(64, 384), vb(128, 256), vm(128, 128),
             vm(2, 4, 8, 128), vm(2, 4, 8, 128), vm(2, 8, 8, 128), vm(2, 8, 8, 128), vm(2, 8, 8, 256), vm(2, 8, 8, 256),
             vm(8, 16, 128), vm(8, 32, 256), vm(4, 64, 128), vm(8, 4, 16, 128),
             vm(4, 64, 512), vm(4, 64, 512), vm(4, 8, 80, 128),
@@ -461,10 +497,10 @@
             pltpu.SemaphoreType.DMA((10,)), pltpu.SemaphoreType.DMA((sems,)), pltpu.SemaphoreType.DMA((sems,)),
         ],
         compiler_params=pltpu.CompilerParams(
-            collective_id=0, has_side_effects=True, vmem_limit_bytes=48 * 1024 * 1024
+            collective_id=0, has_side_effects=True, vmem_limit_bytes=52 * 1024 * 1024
         ),
         name="exchange",
-    )(pressure, *tabs)
+    )(pressure, jnp.asarray(TAB))
     return tuple(
         pl.pallas_call(
             write_kernel,

time: 54.1 us -> 43.1 us (0.80)
  local copies, waits for them, and re-layouts: 9.12 us -> 0 us
  Pallas kernels: 43.8 us -> 42.4 us
    unnamed x18 -> x0, local copies, waits for them, and re-layouts: 9.12 us -> none
    pallas_call x1, Pallas kernels: 41.9 us -> 40.4 us  [per_device(): pl.pallas_call(main_kernel, out_shape=[jax.ShapeDtypeStruct(s, F32) for s...]
where the time goes in v2:
time: 43.1 us; the launch traced here: 43 us
  Pallas kernels  42.4 us (98%)
  between operations  0.64 us (1%)
    pallas_call x1, Pallas kernels, per_device(): pl.pallas_call(main_kernel, out_shape=[jax.ShapeDtypeStruct(s, F32) for s...  40.4 us
    pallas_call x1, Pallas kernels, per_device(): pl.pallas_call(write_kernel, out_shape=[jax.ShapeDtypeStruct(s, F32) for...  1.96 us

profile of v2, /device:TPU:1, one launch (start us, length us, event | category | flops | bytes accessed | tf_op | source)
XLA Modules:
  0.0 43.0 jit_solution(4709198564076542901)
XLA Ops:
  0.6 40.4 %exchange.1 = (f32[7,4,32,256]{3,2,1,0:T(8,128)S(1)}, f32[7,2,16,128]{3,2,1,0:T(8,128)S(1)}, f32[7,1,8,64]{3,2,1,0:T(8,128)S(1)}, f32[64,512]{1,0:T(8,128)S(1)}) custom-call(f32[8,64,512]{2,1,0:T(8,128)} %v_hbm.1, bf16[6784,512]{1,0:T(8,128)(2,1)} %constant.2.clone.tab), custom_call_target="tpu_custom_call" | custom-call | tf_op jit(solution)/shard_map/exchange/pallas_call | solution.py:483
  41.1 2.0 %write.1 = (f32[7,4,32,256]{3,2,1,0:T(8,128)}, f32[7,2,16,128]{3,2,1,0:T(8,128)}, f32[7,1,8,64]{3,2,1,0:T(8,128)}, f32[8,32,4,32]{3,2,1,0:T(4,128)}) custom-call(f32[7,4,32,256]{3,2,1,0:T(8,128)S(1)} %get-tuple-element.8.d1, f32[7,2,16,128]{3,2,1,0:T(8,128)S(1)} %get-tuple-element.9.d2, f32[7,1,8,64]{3,2,1,0:T(8,128)S(1)} %get-tuple-element.10.d3, ...), custom_call_target="tpu_custom_call" | custom-call | tf_op jit(solution)/shard_map/write/pallas_call | solution.py:505

commit v3 on v2

--- a/solution.py
+++ b/solution.py
@@ -96,8 +96,10 @@
 def tables():
     x4 = CH[4].T
     t = {}
-    t["x34"] = stack_rhs(np.concatenate([CH[3].T, x4, x4], axis=1))
-    t["x2"] = stack_rhs(CH[2].T)
+    t["x4"] = stack_rhs(np.concatenate([x4, x4], axis=1))
+    second = lift_matrix(256)
+    third = lift_matrix(128) @ second[:128]
+    t["x23"] = stack_rhs(np.concatenate([second.T, third.T], axis=1))
     t["x1"] = stack_rhs(CH[1].T)
     t["y4"] = np.stack([stack_lhs(y4_table(n)) for n in (0, 3, 7)])
     t["y3"] = np.stack([stack_lhs(y_table(3, n)) for n in range(8)])
@@ -116,16 +118,19 @@
                 assert abs(low3[w, 64 * y : 64 * y + 64]).max() < 1e-15
     t["ca"] = np.stack([stack_lhs(ca[y]) for y in range(8)])
     t["fin"] = stack_lhs(fin)
-    c3 = np.zeros((64, 8, 2, 8))
+    c3 = np.zeros((64, 8, 2, 4))
     for w in range(64):
-        for i in range(8):
+        for i in range(7):
             to = w + i - 3
             if 0 <= to < 64:
-                c3[w, i, 0] = CH[3][to, 8 * w : 8 * w + 8]
-                c3[w, i, 1] = CH[3][64 + to, 8 * w : 8 * w + 8]
+                c3[w, i, 0] = third[to, 4 * w : 4 * w + 4]
+                c3[w, i, 1] = third[64 + to, 4 * w : 4 * w + 4]
+        for to in range(64):
+            if abs(to - w) > 3:
+                assert abs(third[[to, 64 + to], 4 * w : 4 * w + 4]).max() < 1e-15
     for w in range(4, 60):
         assert abs(c3[w] - c3[30]).max() < 1e-15
-    c3 = c3[[0, 1, 2, 3, 30, 60, 61, 62, 63]].reshape(9, 128, 1)
+    c3 = c3[[0, 1, 2, 3, 30, 60, 61, 62, 63]].reshape(9, 64, 1)
     t["c3"] = np.concatenate([np.repeat(h, 128, axis=2) for h in two(c3)], axis=2)
     return t
 
@@ -133,7 +138,7 @@
 def pack(t):
     blocks = {
         "x1": t["x1"],
-        "xs": np.concatenate([t["x34"], t["x2"]], axis=1),
+        "xs": np.concatenate([t["x4"], np.pad(t["x23"], ((0, 768), (0, 0)))], axis=1),
         "y4": t["y4"].reshape(3, 192, 3, 512).transpose(0, 2, 1, 3).reshape(-1, 512),
         "y2": t["y2"].reshape(-1, 192),
         "y3": t["y3"].reshape(-1, 192),
@@ -194,8 +199,8 @@
 
 def main_kernel(v_hbm, tab,
                 d1_o, d2_o, d3_o, f_o,
-                v, vc, x34, y4, x2, y3, y2, x1, ca, fin, c3b, c3,
-                so4, ri4, so3, ri3, so2, ri2, t3, t2, ga, gb, st1, zh1, e1, st2, zh2, t2b, st2b, zh2b, s3, r3,
+                raw, v, vc, x4, y4, x23, y3, y2, x1, ca, fin, c3b, c3,
+                so4, ri4, so23, ri23, t3, t2, ga, gb, st1, zh1, e1, st2, zh2, s3, r3,
                 lsem, ss, rs):
     w, n = lax.axis_index("wide"), lax.axis_index("narrow")
     y, z = w // 8, w % 8
@@ -204,7 +209,7 @@
     n_up, n_dn = (n + 1) % 8, (n + 7) % 8
     w_up, w_dn = (w + 1) % 64, (w + 63) % 64
 
-    loads = [pltpu.make_async_copy(v_hbm, v, lsem.at[0])]
+    loads = [pltpu.make_async_copy(v_hbm, raw, lsem.at[0])]
 
     def load(name, index, dst, lane=0):
         rows, lanes = dst.shape
@@ -217,21 +222,21 @@
         return c
 
     l_v = loads[0]
-    l_x34 = load("xs", 0, x34)
+    l_x4 = load("xs", 0, x4)
     l_y4 = load("y4", jnp.minimum(n, 1) + n // 7, y4)
-    l_x2 = load("xs", 0, x2, 256)
+    l_x1 = load("x1", 0, x1)
+    l_x23 = load("xs", 0, x23, 128)
     l_y3 = load("y3", n, y3)
     l_y2 = load("y2", n, y2)
+    l_ca = load("ca", y, ca)
     l_c3 = load("c3", jnp.minimum(w, 4) + jnp.maximum(w - 59, 0), c3b)
-    l_ca = load("ca", y, ca)
-    l_x1 = load("x1", 0, x1)
     l_fin = load("fin", 0, fin)
     for c in loads:
         c.start()
 
     barrier = pltpu.get_barrier_semaphore()
     peers = [(w, n_up), (w, n_dn)]
-    peers += [((w + 64 + d) % 64, n) for d in (1, -1, 2, -2, 3, -3, 4, -4)]
+    peers += [((w + 64 + d) % 64, n) for d in (1, -1, 2, -2, 3, -3)]
     peers += [(y * 8 + (z + d) % 8, n) for d in range(1, 8)]
     peers += [(((y + d) % 8) * 8 + z, n) for d in range(1, 8)]
     for p in peers:
@@ -251,14 +256,13 @@
         return c
 
     l_v.wait()
-    hi, lo = halves(v[...].reshape(512, 512))
+    hi, lo = halves(raw[...].reshape(512, 512))
     vc[:, 0:512] = hi
     vc[:, 512:1024] = lo
     vc[:, 1024:1536] = hi
-    l_x34.wait()
-    xa = dot(vc[...], x34[...])
+    l_x4.wait()
+    hi, lo = halves(dot(vc[...], x4[...]))
     l_y4.wait()
-    hi, lo = halves(xa[:, 128:256])
     o4 = dot(y4[0:192], hi) + dot(y4[192:384], lo) + dot(y4[384:576], hi)
     o4 = o4.reshape(24, 8, 128)
     lane_low = lax.broadcasted_iota(jnp.int32, (8, 128), 1) < 64
@@ -274,29 +278,18 @@
     pl.semaphore_wait(barrier, len(peers))
     a4 = [send(so4.at[0], ri4.at[0], (w, n_up)), send(so4.at[1], ri4.at[1], (w, n_dn))]
 
-    (q0, q1), (q2, q3) = z_states([v[i] for i in range(8)])
-    st1[0], st1[1], st1[2], st1[3] = q0, q1, q2, q3
-    a1 = [
-        send(st1.at[pl.ds(0, 2)], zh1.at[pl.ds(0, 2)], (w_dn, n)),
-        send(st1.at[pl.ds(2, 2)], zh1.at[pl.ds(2, 2)], (w_up, n)),
-    ]
-
-    l_y3.wait()
-    for p in range(8):
-        o = dot(y3[:, 0:192], data_rhs(xa[64 * p : 64 * p + 64, 0:128]))
-        t3[p] = o[0:16]
-        so3[0, p] = o[16:24]
-        so3[1, p] = o[24:32]
-    a3 = [send(so3.at[0], ri3.at[0], (w, n_up)), send(so3.at[1], ri3.at[1], (w, n_dn))]
-    l_x2.wait()
-    l_y2.wait()
-    xb = dot(vc[...], x2[...])
-    for p in range(8):
-        o = dot(y2[:, 0:192], data_rhs(xb[64 * p : 64 * p + 64]))
-        t2[p] = o[0:32]
-        so2[0, p] = o[32:40]
-        so2[1, p] = o[40:48]
-    a2 = [send(so2.at[0], ri2.at[0], (w, n_up)), send(so2.at[1], ri2.at[1], (w, n_dn))]
+    l_x1.wait()
+    a1 = []
+    for h in range(2):
+        v[h] = dot(vc[...], x1[:, 256 * h : 256 * h + 256]).reshape(8, 64, 256)
+        (q0, q1), (q2, q3) = z_states([v[h, i] for i in range(8)])
+        st1[h, 0], st1[h, 1], st1[h, 2], st1[h, 3] = q0, q1, q2, q3
+        a1.append(
+            [
+                send(st1.at[h, pl.ds(0, 2)], zh1.at[h, pl.ds(0, 2)], (w_dn, n)),
+                send(st1.at[h, pl.ds(2, 2)], zh1.at[h, pl.ds(2, 2)], (w_up, n)),
+            ]
+        )
 
     for c in a4:
         c.wait_recv()
@@ -308,27 +301,45 @@
         send(ga.at[:, here, :], ga.at[:, here, :], (y * 8 + (z + d) % 8, n)) for d in (4, 3, 5, 2, 6, 1, 7)
     ]
 
-    def add_parts(t, ri, own):
-        width = t.shape[-1]
-        sub_low = lax.broadcasted_iota(jnp.int32, (8, width), 0) < 4
-        for p in range(8):
-            up = jnp.where(nfirst, 0.0, ri[0, p])
-            dn = jnp.where(nlast, 0.0, ri[1, p])
-            up_r, dn_r = pltpu.roll(up, 4, 0), pltpu.roll(dn, 4, 0)
-            t[p, 0:8] = t[p, 0:8] + jnp.where(sub_low, up, 0.0)
-            t[p, own : own + 8] = t[p, own : own + 8] + jnp.where(sub_low, up_r, 0.0)
-            t[p, own - 8 : own] = t[p, own - 8 : own] + jnp.where(sub_low, 0.0, dn)
-            t[p, 2 * own - 8 : 2 * own] = t[p, 2 * own - 8 : 2 * own] + jnp.where(sub_low, 0.0, dn_r)
-
-    for c in a2:
-        c.wait_recv()
-    add_parts(t2, ri2, 16)
-    (q0, q1), (q2, q3) = z_states([t2[i] for i in range(8)])
-    st2[0], st2[1], st2[2], st2[3] = q0, q1, q2, q3
-    b2 = [
-        send(st2.at[pl.ds(0, 2)], zh2.at[pl.ds(0, 2)], (w_dn, n)),
-        send(st2.at[pl.ds(2, 2)], zh2.at[pl.ds(2, 2)], (w_up, n)),
-    ]
+    def z_of_half(h):
+        for c in a1[h]:
+            c.wait_recv()
+        for q in range(8):
+            rows = slice(8 * q, 8 * q + 8)
+            low, high = z_lift(
+                [v[h, i, rows] for i in range(8)],
+                zh1[h, 0, rows], zh1[h, 1, rows], zh1[h, 2, rows], zh1[h, 3, rows], wfirst, wlast, True,
+            )
+            both = low + high
+            for i in range(8):
+                v[h, i, rows] = both[i]
+
+    def y_halo(h):
+        for q in range(2):
+            e1[2 * h + q, :, 8:72, :] = v[h, :, :, 128 * q : 128 * q + 128]
+        part = e1.at[pl.ds(2 * h, 2)]
+        return [
+            send(part.at[:, :, pl.ds(64, 8), :], part.at[:, :, pl.ds(0, 8), :], (w, n_up)),
+            send(part.at[:, :, pl.ds(8, 8), :], part.at[:, :, pl.ds(72, 8), :], (w, n_dn)),
+        ]
+
+    z_of_half(0)
+    l_x23.wait()
+    hi, lo = halves(v[0, 0:4].reshape(256, 256))
+    xb = dot(jnp.concatenate([hi, lo, hi], axis=1), x23[...])
+    l_y2.wait()
+    l_y3.wait()
+    for p in range(4):
+        o = dot(y2[:, 0:192], data_rhs(xb[64 * p : 64 * p + 64, 0:256]))
+        t2[p] = o[0:32]
+        so23[0, p, :, 0:256] = o[32:40]
+        so23[1, p, :, 0:256] = o[40:48]
+        o = dot(y3[:, 0:192], data_rhs(xb[64 * p : 64 * p + 64, 256:384]))
+        t3[p] = o[0:16]
+        so23[0, p, :, 256:384] = o[16:24]
+        so23[1, p, :, 256:384] = o[24:32]
+    a23 = [send(so23.at[0], ri23.at[0], (w, n_up)), send(so23.at[1], ri23.at[1], (w, n_dn))]
+    c1 = [y_halo(0)]
 
     l_ca.wait()
     for c in ga_sends:
@@ -339,94 +350,84 @@
         gb[y, r] = part[:, 128 * r : 128 * r + 128]
     gb_sends = [send(gb.at[y], gb.at[y], (((y + d) % 8) * 8 + z, n)) for d in (4, 3, 5, 2, 6, 1, 7)]
 
-    for c in a1:
+    def add_parts(t, cols, own):
+        sub_low = lax.broadcasted_iota(jnp.int32, (8, t.shape[-1]), 0) < 4
+        for p in range(4):
+            up = jnp.where(nfirst, 0.0, ri23[0, p, :, cols])
+            dn = jnp.where(nlast, 0.0, ri23[1, p, :, cols])
+            up_r, dn_r = pltpu.roll(up, 4, 0), pltpu.roll(dn, 4, 0)
+            t[p, 0:8] = t[p, 0:8] + jnp.where(sub_low, up, 0.0)
+            t[p, own : own + 8] = t[p, own : own + 8] + jnp.where(sub_low, up_r, 0.0)
+            t[p, own - 8 : own] = t[p, own - 8 : own] + jnp.where(sub_low, 0.0, dn)
+            t[p, 2 * own - 8 : 2 * own] = t[p, 2 * own - 8 : 2 * own] + jnp.where(sub_low, 0.0, dn_r)
+
+    for c in a23:
         c.wait_recv()
-    for q in range(8):
-        rows = slice(8 * q, 8 * q + 8)
-        low, high = z_lift(
-            [v[i, rows] for i in range(8)], zh1[0, rows], zh1[1, rows], zh1[2, rows], zh1[3, rows], wfirst, wlast, True
-        )
-        for i in range(4):
-            v[i, rows] = low[i]
-            v[4 + i, rows] = high[i]
-    hi, lo = halves(v[...].reshape(512, 512))
-    vc[:, 0:512] = hi
-    vc[:, 512:1024] = lo
-    vc[:, 1024:1536] = hi
-    l_x1.wait()
-    for h in range(2):
-        o = dot(vc[...], x1[:, 256 * h : 256 * h + 256]).reshape(8, 64, 256)
-        for q in range(2):
-            e1[2 * h + q, :, 8:72, :] = o[:, :, 128 * q : 128 * q + 128]
-    c1 = [
-        send(e1.at[:, :, pl.ds(64, 8), :], e1.at[:, :, pl.ds(0, 8), :], (w, n_up)),
-        send(e1.at[:, :, pl.ds(8, 8), :], e1.at[:, :, pl.ds(72, 8), :], (w, n_dn)),
+    add_parts(t2, slice(0, 256), 16)
+    add_parts(t3, slice(256, 384), 8)
+    (q0, q1), (q2, q3) = z_states([t2[i] for i in range(4)])
+    st2[0], st2[1], st2[2], st2[3] = q0, q1, q2, q3
+    b2 = [
+        send(st2.at[pl.ds(0, 2)], zh2.at[pl.ds(0, 2)], (w_dn, n)),
+        send(st2.at[pl.ds(2, 2)], zh2.at[pl.ds(2, 2)], (w_up, n)),
     ]
-
-    for c in b2:
-        c.wait_recv()
-    low, _ = z_lift([t2[i] for i in range(8)], zh2[0], zh2[1], zh2[2], zh2[3], wfirst, wlast, False)
-    (q0, q1), (q2, q3) = z_states(low)
-    for i in range(4):
-        t2b[i] = low[i]
-    st2b[0], st2b[1], st2b[2], st2b[3] = q0, q1, q2, q3
-    c2 = [
-        send(st2b.at[pl.ds(0, 2)], zh2b.at[pl.ds(0, 2)], (w_dn, n)),
-        send(st2b.at[pl.ds(2, 2)], zh2b.at[pl.ds(2, 2)], (w_up, n)),
-    ]
-
-    for c in a3:
-        c.wait_recv()
-    add_parts(t3, ri3, 8)
     l_c3.wait()
     c3[...] = c3b[:, 0:128].astype(F32) + c3b[:, 128:256].astype(F32)
-    planes3 = [t3[p] for p in range(8)]
+    planes3 = [t3[p] for p in range(4)]
     b3 = []
-    for i in (7, 6, 5, 4, 2, 1, 0, 3):
+    for i in (6, 0, 5, 1, 4, 2, 3):
         for j in range(2):
-            k = i * 16 + j * 8
+            k = i * 8 + j * 4
             acc = planes3[0] * c3[k : k + 1]
-            for p in range(1, 8):
+            for p in range(1, 4):
                 acc = acc + planes3[p] * c3[k + p : k + p + 1]
             s3[i, j] = acc
         if i != 3:
             b3.append(send(s3.at[i], r3.at[i], ((w + 64 + i - 3) % 64, n)))
 
-    for c in c1:
-        c.wait_recv()
-
-    @pl.when(nfirst)
-    def _():
-        for k in range(1, 5):
-            e1[:, :, 8 - k : 9 - k, :] = e1[:, :, 8 + k : 9 + k, :]
-
-    @pl.when(nlast)
-    def _():
-        for k in range(1, 5):
-            e1[:, :, 71 + k : 72 + k, :] = e1[:, :, 71 - k : 72 - k, :]
+    z_of_half(1)
+    c1.append(y_halo(1))
 
     def tap(c, i, off):
         return e1[c, i, pl.ds(8 + off, 32, stride=2), :]
 
-    for i in range(8):
-        bz, zz = i // 4, i % 4
-        for c in range(4):
-            bx, cols = c // 2, slice(128 * (c % 2), 128 * (c % 2) + 128)
-            if bz or bx:
-                low = H_LOW[0] * tap(c, i, 0)
-                for k in range(1, 5):
-                    low = low + H_LOW[k] * (tap(c, i, -k) + tap(c, i, k))
-                d1_o[4 * bz + bx - 1, zz, :, cols] = low
-            high = H_HIGH[0] * tap(c, i, 1)
-            for k in range(1, 4):
-                high = high + H_HIGH[k] * (tap(c, i, 1 - k) + tap(c, i, 1 + k))
-            d1_o[4 * bz + 2 + bx - 1, zz, :, cols] = high
+    def bands_one(h):
+        for c in c1[h]:
+            c.wait_recv()
+        own = slice(2 * h, 2 * h + 2)
+
+        @pl.when(nfirst)
+        def _():
+            for k in range(1, 5):
+                e1[own, :, 8 - k : 9 - k, :] = e1[own, :, 8 + k : 9 + k, :]
+
+        @pl.when(nlast)
+        def _():
+            for k in range(1, 5):
+                e1[own, :, 71 + k : 72 + k, :] = e1[own, :, 71 - k : 72 - k, :]
+
+        for i in range(8):
+            bz, zz = i // 4, i % 4
+            for q in range(2):
+                c, cols = 2 * h + q, slice(128 * q, 128 * q + 128)
+                if bz or h:
+                    low = H_LOW[0] * tap(c, i, 0)
+                    for k in range(1, 5):
+                        low = low + H_LOW[k] * (tap(c, i, -k) + tap(c, i, k))
+                    d1_o[4 * bz + h - 1, zz, :, cols] = low
+                high = H_HIGH[0] * tap(c, i, 1)
+                for k in range(1, 4):
+                    high = high + H_HIGH[k] * (tap(c, i, 1 - k) + tap(c, i, 1 + k))
+                d1_o[4 * bz + 2 + h - 1, zz, :, cols] = high
+
+    bands_one(0)
+    bands_one(1)
 
     for c in b3:
         c.wait_recv()
     for j in range(2):
         acc = s3[3, j]
-        for i in range(8):
+        for i in range(7):
             if i != 3:
                 src = w - (i - 3)
                 acc = acc + jnp.where((src >= 0) & (src < 64), r3[i, j], 0.0)
@@ -437,9 +438,9 @@
                 cols = slice(64 * (b % 2), 64 * (b % 2) + 64)
                 d3_o[band - 1, 0] = acc[rows, cols]
 
-    for c in c2:
+    for c in b2:
         c.wait_recv()
-    low, high = z_lift([t2b[i] for i in range(4)], zh2b[0], zh2b[1], zh2b[2], zh2b[3], wfirst, wlast, True)
+    low, high = z_lift([t2[i] for i in range(4)], zh2[0], zh2[1], zh2[2], zh2[3], wfirst, wlast, True)
     for band in range(1, 8):
         src = high if band >= 4 else low
         by, bx = (band // 2) % 2, band % 2
@@ -486,14 +487,14 @@
         in_specs=[ANY] * 2,
         out_specs=[VM] * 4,
         scratch_shapes=[
-            vm(8, 64, 512), vb(512, 1536),
-            vb(1536, 256), vb(576, 512), vb(1536, 256), vb(32, 256), vb(48, 256), vb(1536, 512),
-            vb(16, 256), vb(64, 384), vb(128, 256), vm(128, 128),
-            vm(2, 4, 8, 128), vm(2, 4, 8, 128), vm(2, 8, 8, 128), vm(2, 8, 8, 128), vm(2, 8, 8, 256), vm(2, 8, 8, 256),
-            vm(8, 16, 128), vm(8, 32, 256), vm(4, 64, 128), vm(8, 4, 16, 128),
-            vm(4, 64, 512), vm(4, 64, 512), vm(4, 8, 80, 128),
-            vm(4, 32, 256), vm(4, 32, 256), vm(4, 32, 256), vm(4, 32, 256), vm(4, 32, 256),
-            vm(8, 2, 16, 128), vm(8, 2, 16, 128),
+            vm(8, 64, 512), vm(2, 8, 64, 256), vb(512, 1536),
+            vb(1536, 128), vb(576, 512), vb(768, 384), vb(32, 256), vb(48, 256), vb(1536, 512),
+            vb(16, 256), vb(64, 384), vb(64, 256), vm(64, 128),
+            vm(2, 4, 8, 128), vm(2, 4, 8, 128), vm(2, 4, 8, 384), vm(2, 4, 8, 384),
+            vm(4, 16, 128), vm(4, 32, 256), vm(4, 64, 128), vm(8, 4, 16, 128),
+            vm(2, 4, 64, 256), vm(2, 4, 64, 256), vm(4, 8, 80, 128),
+            vm(4, 32, 256), vm(4, 32, 256),
+            vm(7, 2, 16, 128), vm(7, 2, 16, 128),
             pltpu.SemaphoreType.DMA((10,)), pltpu.SemaphoreType.DMA((sems,)), pltpu.SemaphoreType.DMA((sems,)),
         ],
         compiler_params=pltpu.CompilerParams(

time: 43.1 us -> 41.2 us (0.956)
  Pallas kernels: 42.4 us -> 40.4 us
    pallas_call x1, Pallas kernels: 40.4 us -> 38.5 us  [per_device(): pl.pallas_call(main_kernel, out_shape=[jax.ShapeDtypeStruct(s, F32) for s...]
where the time goes in v3:
time: 41.2 us; the launch traced here: 41.1 us
  Pallas kernels  40.4 us (98%)
  between operations  0.64 us (2%)
    pallas_call x1, Pallas kernels, per_device(): pl.pallas_call(main_kernel, out_shape=[jax.ShapeDtypeStruct(s, F32) for s...  38.5 us
    pallas_call x1, Pallas kernels, per_device(): pl.pallas_call(write_kernel, out_shape=[jax.ShapeDtypeStruct(s, F32) for...  1.96 us

profile of v3, /device:TPU:1, one launch (start us, length us, event | category | flops | bytes accessed | tf_op | source)
XLA Modules:
  0.0 41.1 jit_solution(11353900352966809162)
XLA Ops:
  0.6 38.5 %exchange.1 = (f32[7,4,32,256]{3,2,1,0:T(8,128)S(1)}, f32[7,2,16,128]{3,2,1,0:T(8,128)S(1)}, f32[7,1,8,64]{3,2,1,0:T(8,128)S(1)}, f32[64,512]{1,0:T(8,128)S(1)}) custom-call(f32[8,64,512]{2,1,0:T(8,128)} %v_hbm.1, bf16[6208,512]{1,0:T(8,128)(2,1)} %constant.2.clone.tab), custom_call_target="tpu_custom_call" | custom-call | tf_op jit(solution)/shard_map/exchange/pallas_call | solution.py:484
  39.1 2.0 %write.1 = (f32[7,4,32,256]{3,2,1,0:T(8,128)}, f32[7,2,16,128]{3,2,1,0:T(8,128)}, f32[7,1,8,64]{3,2,1,0:T(8,128)}, f32[8,32,4,32]{3,2,1,0:T(4,128)}) custom-call(f32[7,4,32,256]{3,2,1,0:T(8,128)S(1)} %get-tuple-element.8.d1, f32[7,2,16,128]{3,2,1,0:T(8,128)S(1)} %get-tuple-element.9.d2, f32[7,1,8,64]{3,2,1,0:T(8,128)S(1)} %get-tuple-element.10.d3, ...), custom_call_target="tpu_custom_call" | custom-call | tf_op jit(solution)/shard_map/write/pallas_call | solution.py:506

commit v4 on v3

--- a/solution.py
+++ b/solution.py
@@ -125,6 +125,7 @@
             if 0 <= to < 64:
                 c3[w, i, 0] = third[to, 4 * w : 4 * w + 4]
                 c3[w, i, 1] = third[64 + to, 4 * w : 4 * w + 4]
+        assert abs(c3[w, 6, 1]).max() < 1e-15
         for to in range(64):
             if abs(to - w) > 3:
                 assert abs(third[[to, 64 + to], 4 * w : 4 * w + 4]).max() < 1e-15
@@ -278,18 +279,17 @@
     pl.semaphore_wait(barrier, len(peers))
     a4 = [send(so4.at[0], ri4.at[0], (w, n_up)), send(so4.at[1], ri4.at[1], (w, n_dn))]
 
-    l_x1.wait()
-    a1 = []
-    for h in range(2):
+    def z_send(h):
         v[h] = dot(vc[...], x1[:, 256 * h : 256 * h + 256]).reshape(8, 64, 256)
         (q0, q1), (q2, q3) = z_states([v[h, i] for i in range(8)])
         st1[h, 0], st1[h, 1], st1[h, 2], st1[h, 3] = q0, q1, q2, q3
-        a1.append(
-            [
-                send(st1.at[h, pl.ds(0, 2)], zh1.at[h, pl.ds(0, 2)], (w_dn, n)),
-                send(st1.at[h, pl.ds(2, 2)], zh1.at[h, pl.ds(2, 2)], (w_up, n)),
-            ]
-        )
+        return [
+            send(st1.at[h, pl.ds(0, 2)], zh1.at[h, pl.ds(0, 2)], (w_dn, n)),
+            send(st1.at[h, pl.ds(2, 2)], zh1.at[h, pl.ds(2, 2)], (w_up, n)),
+        ]
+
+    l_x1.wait()
+    a1 = [z_send(0)]
 
     for c in a4:
         c.wait_recv()
@@ -298,7 +298,7 @@
         add = jnp.where(nfirst, 0.0, ri4[0, r]) + jnp.where(nlast, 0.0, ri4[1, r])
         ga[r, here, :] = own4[r] + add
     ga_sends = [
-        send(ga.at[:, here, :], ga.at[:, here, :], (y * 8 + (z + d) % 8, n)) for d in (4, 3, 5, 2, 6, 1, 7)
+        send(ga.at[:, here, :], ga.at[:, here, :], (y * 8 + (z + d) % 8, n)) for d in (1, 7, 2, 6, 3, 5, 4)
     ]
 
     def z_of_half(h):
@@ -341,6 +341,8 @@
     a23 = [send(so23.at[0], ri23.at[0], (w, n_up)), send(so23.at[1], ri23.at[1], (w, n_dn))]
     c1 = [y_halo(0)]
 
+    a1.append(z_send(1))
+
     l_ca.wait()
     for c in ga_sends:
         c.wait_recv()
@@ -348,7 +350,7 @@
     part = dot(ca[:, 0:192], data_rhs(cat))
     for r in range(4):
         gb[y, r] = part[:, 128 * r : 128 * r + 128]
-    gb_sends = [send(gb.at[y], gb.at[y], (((y + d) % 8) * 8 + z, n)) for d in (4, 3, 5, 2, 6, 1, 7)]
+    gb_sends = [send(gb.at[y], gb.at[y], (((y + d) % 8) * 8 + z, n)) for d in (1, 7, 2, 6, 3, 5, 4)]
 
     def add_parts(t, cols, own):
         sub_low = lax.broadcasted_iota(jnp.int32, (8, t.shape[-1]), 0) < 4
@@ -383,7 +385,8 @@
                 acc = acc + planes3[p] * c3[k + p : k + p + 1]
             s3[i, j] = acc
         if i != 3:
-            b3.append(send(s3.at[i], r3.at[i], ((w + 64 + i - 3) % 64, n)))
+            kept = pl.ds(0, 1 if i == 6 else 2)
+            b3.append(send(s3.at[i, kept], r3.at[i, kept], ((w + 64 + i - 3) % 64, n)))
 
     z_of_half(1)
     c1.append(y_halo(1))
@@ -428,7 +431,7 @@
     for j in range(2):
         acc = s3[3, j]
         for i in range(7):
-            if i != 3:
+            if i != 3 and not (j and i == 6):
                 src = w - (i - 3)
                 acc = acc + jnp.where((src >= 0) & (src < 64), r3[i, j], 0.0)
         for b in range(4):
@@ -466,9 +469,11 @@
             tile = f[32 * bz : 32 * bz + 32, 128 * r : 128 * r + 128]
             for b in range(4):
                 buf[4 * bz + b, :, r, :] = tile[:, 32 * b : 32 * b + 32]
-    last = pltpu.make_async_copy(buf, o4, sem.at[3])
-    last.start()
-    for c in copies + [last]:
+        half = pl.ds(4 * bz, 4)
+        c = pltpu.make_async_copy(buf.at[half], o4.at[half], sem.at[3 + bz])
+        c.start()
+        copies.append(c)
+    for c in copies:
         c.wait()
 
 
@@ -508,7 +513,7 @@
             out_shape=[jax.ShapeDtypeStruct(s, F32) for s in OUTS],
             in_specs=[VM] * 4,
             out_specs=[ANY] * 4,
-            scratch_shapes=[pltpu.VMEM(OUTS[3], F32), pltpu.SemaphoreType.DMA((4,))],
+            scratch_shapes=[pltpu.VMEM(OUTS[3], F32), pltpu.SemaphoreType.DMA((5,))],
             compiler_params=pltpu.CompilerParams(vmem_limit_bytes=16 * 1024 * 1024),
             name="write",
         )(*mid)

time: 41.2 us -> 39.3 us (0.954)
  Pallas kernels: 40.4 us -> 38.3 us
    pallas_call x1, Pallas kernels: 38.5 us -> 36.7 us  [per_device(): pl.pallas_call(main_kernel, out_shape=[jax.ShapeDtypeStruct(s, F32) for s...]
where the time goes in v4:
time: 39.3 us; the launch traced here: 39 us
  Pallas kernels  38.3 us (97%)
  between operations  0.64 us (2%)
    pallas_call x1, Pallas kernels, per_device(): pl.pallas_call(main_kernel, out_shape=[jax.ShapeDtypeStruct(s, F32) for s...  36.7 us
    pallas_call x1, Pallas kernels, per_device(): pl.pallas_call(write_kernel, out_shape=[jax.ShapeDtypeStruct(s, F32) for...  1.63 us

profile of v4, /device:TPU:1, one launch (start us, length us, event | category | flops | bytes accessed | tf_op | source)
XLA Modules:
  0.0 39.0 jit_solution(17859336455410546646)
XLA Ops:
  0.6 36.7 %exchange.1 = (f32[7,4,32,256]{3,2,1,0:T(8,128)S(1)}, f32[7,2,16,128]{3,2,1,0:T(8,128)S(1)}, f32[7,1,8,64]{3,2,1,0:T(8,128)S(1)}, f32[64,512]{1,0:T(8,128)S(1)}) custom-call(f32[8,64,512]{2,1,0:T(8,128)} %v_hbm.1, bf16[6208,512]{1,0:T(8,128)(2,1)} %constant.2.clone.tab), custom_call_target="tpu_custom_call" | custom-call | tf_op jit(solution)/shard_map/exchange/pallas_call | solution.py:489
  37.3 1.6 %write.1 = (f32[7,4,32,256]{3,2,1,0:T(8,128)}, f32[7,2,16,128]{3,2,1,0:T(8,128)}, f32[7,1,8,64]{3,2,1,0:T(8,128)}, f32[8,32,4,32]{3,2,1,0:T(4,128)}) custom-call(f32[7,4,32,256]{3,2,1,0:T(8,128)S(1)} %get-tuple-element.8.d1, f32[7,2,16,128]{3,2,1,0:T(8,128)S(1)} %get-tuple-element.9.d2, f32[7,1,8,64]{3,2,1,0:T(8,128)S(1)} %get-tuple-element.10.d3, ...), custom_call_target="tpu_custom_call" | custom-call | tf_op jit(solution)/shard_map/write/pallas_call | solution.py:511

commit v5 on v4

--- a/solution.py
+++ b/solution.py
@@ -377,7 +377,7 @@
     c3[...] = c3b[:, 0:128].astype(F32) + c3b[:, 128:256].astype(F32)
     planes3 = [t3[p] for p in range(4)]
     b3 = []
-    for i in (6, 0, 5, 1, 4, 2, 3):
+    for i in (4, 2, 5, 1, 6, 0, 3):
         for j in range(2):
             k = i * 8 + j * 4
             acc = planes3[0] * c3[k : k + 1]

time: 39.3 us -> 39 us (level)
  the two profiles are of different devices: /device:TPU:1 before, /device:TPU:2 now
where the time goes in v5:
time: 39 us; the launch traced here: 38.9 us
  Pallas kernels  38.3 us (98%)
  between operations  0.64 us (2%)
    pallas_call x1, Pallas kernels, per_device(): pl.pallas_call(main_kernel, out_shape=[jax.ShapeDtypeStruct(s, F32) for s...  36.6 us
    pallas_call x1, Pallas kernels, per_device(): pl.pallas_call(write_kernel, out_shape=[jax.ShapeDtypeStruct(s, F32) for...  1.63 us

profile of v5, /device:TPU:2, one launch (start us, length us, event | category | flops | bytes accessed | tf_op | source)
XLA Modules:
  0.0 38.9 jit_solution(11426252157224951761)
XLA Ops:
  0.6 36.6 %exchange.1 = (f32[7,4,32,256]{3,2,1,0:T(8,128)S(1)}, f32[7,2,16,128]{3,2,1,0:T(8,128)S(1)}, f32[7,1,8,64]{3,2,1,0:T(8,128)S(1)}, f32[64,512]{1,0:T(8,128)S(1)}) custom-call(f32[8,64,512]{2,1,0:T(8,128)} %v_hbm.1, bf16[6208,512]{1,0:T(8,128)(2,1)} %constant.2.clone.tab), custom_call_target="tpu_custom_call" | custom-call | tf_op jit(solution)/shard_map/exchange/pallas_call | solution.py:489
  37.3 1.6 %write.1 = (f32[7,4,32,256]{3,2,1,0:T(8,128)}, f32[7,2,16,128]{3,2,1,0:T(8,128)}, f32[7,1,8,64]{3,2,1,0:T(8,128)}, f32[8,32,4,32]{3,2,1,0:T(4,128)}) custom-call(f32[7,4,32,256]{3,2,1,0:T(8,128)S(1)} %get-tuple-element.8.d1, f32[7,2,16,128]{3,2,1,0:T(8,128)S(1)} %get-tuple-element.9.d2, f32[7,1,8,64]{3,2,1,0:T(8,128)S(1)} %get-tuple-element.10.d3, ...), custom_call_target="tpu_custom_call" | custom-call | tf_op jit(solution)/shard_map/write/pallas_call | solution.py:511
